TPU v7x, 32 devices: a whole 2x2x4 slice. The times are simulated.
32 devices in a mesh: tiles: 8 (over z, x), ens: 4 (over y, core).
Axes of the slice: x: 2, y: 2, z: 4, core: 2. Of those that a mesh axis runs over, the one named last changes fastest.
Arguments:
- depth: float32 [8, 128, 16384], P('ens', 'tiles'), may hold values from 0.3 to 1.5
- bed: float32 [128, 16384], P('tiles'), may hold values from -1.5 to 1.5
- rain: float32 [8, 128, 16384], P('ens', 'tiles'), may hold values from 0.005 to 0.05
- rough_class: int32 [128, 16384], P('tiles'), may hold values from 0 to 15
- class_n: float32 [16], replicated, may hold values from 0.5 to 2
- contact_seg: int32 [8, 8, 8], P('tiles'), may hold values from 0 to 1023, as said below
- contact_lake: int32 [8, 8, 8], P('tiles'), may hold values from -1 to 319, as said below
- lake_slot: int32 [320], replicated, may hold values from 0 to 319, as said below
- storage: float32 [8, 320], P('ens', 'tiles'), may hold values from 0.5 to 3
- area: float32 [320], P('tiles'), may hold values from 1 to 4
- release: float32 [320], P('tiles'), may hold values from 0.5 to 0.98
- upstream_link: int32 [320], P('tiles'), may hold values from 0 to 1, as said below
Outputs:
- new_depth: float32 [8, 128, 16384], P('ens', 'tiles')
- new_storage: float32 [8, 320], P('ens', 'tiles')
- ens_outflow: float32 [320], P('tiles')
Inputs may be any that keep to these rules, and one draw needn't show every extreme that they name: `contact_seg`: within one source tile the segments of all contact slots are distinct. `contact_lake`: A live entry [d, e, c] names a lake whose slot lake_slot lies on owner tile e (slots e * 40 onward); at most 8 live contacts go from one tile to one owner, and some owner receives 8 from every tile. `lake_slot`: A permutation of the slots. `upstream_link`: slots with index below 40 have 0; runs of linked slots form cascades of at most 8 reservoirs, and one cascade has exactly 8.
All inputs are finite; a program needn't handle non-finite values.
Results may differ from a plain program's by a relative error of at most 0.0001.
Values sent between devices are 32-bit elements; how exact they have to be, the bound alone decides.
No kernel may reach another device: no remote copies, remote signals or barrier semaphores. Data moves between devices by JAX's collectives and lax.ppermute only.
A program may use at most 64 MiB of HBM per device.

v0:
```python
import functools
import types

import jax
import jax.numpy as jnp
from jax import lax
from jax.experimental import pallas as pl
from jax.experimental.pallas import tpu as pltpu
from jax.sharding import PartitionSpec as P

SEG = 256
STEPS = 4
LANES = 128
SUBLANES = 8
FAR = 1e30

flow_rate = 0.035
drain_rate = 0.4

F32 = jnp.float32
I32 = jnp.int32
VMEM_LIMIT = 40 * 2**20
BLOCK = 4096


def up_to(value, unit):
    return -(-value // unit) * unit


def lane_ids(shape):
    return lax.broadcasted_iota(I32, shape, len(shape) - 1)


def row_ids(shape):
    return lax.broadcasted_iota(I32, shape, len(shape) - 2)


def mobility(water, inv_n):
    return water * jnp.exp2(jnp.log2(jnp.abs(water)) * (2.0 / 3.0)) * inv_n


def taken_of(water, surface, level):
    excess = jnp.maximum(surface - level, 0.0)
    return drain_rate * water * excess / (1.0 + excess)


class Array:
    def __init__(self, kernel, h, v):
        self.kernel, self.h, self.v = kernel, h, v

    def load(self):
        self.coming = self.kernel.copy(self.h, self.v)

    def wait(self):
        self.coming.wait()

    def send(self):
        self.kernel.stores.append(self.kernel.copy(self.v, self.h))


class Kernel:
    def __init__(self, sems):
        self.sems, self.count, self.stores = sems, 0, []

    def copy(self, source, target):
        copy = pltpu.make_async_copy(source, target, self.sems.at[self.count])
        self.count += 1
        copy.start()
        return copy

    def finish(self):
        for copy in self.stores:
            copy.wait()


def load(*arrays):
    for array in arrays:
        array.load()


def wait(*arrays):
    for array in arrays:
        array.wait()


def send(*arrays):
    for array in arrays:
        array.send()


class Staged:
    space = pltpu.VMEM

    def __init__(self, x):
        self.x = x


class Scalars(Staged):
    space = pltpu.SMEM


class Raw(Staged):
    space = None


class Here(Staged):
    space = None


def staged_call(body, z, ins, outs, scratch=None, alias=None, extra_sems=0, micros=60):
    scratch = scratch or {}
    ins = {n: x if isinstance(x, Staged) else Staged(x) for n, x in ins.items()}
    outs = {n: x if isinstance(x, Raw) else Staged(x) for n, x in outs.items()}
    shapes = [x.space(x.x.shape, x.x.dtype) for x in ins.values() if x.space]
    shapes += [x.space(x.x, F32) for x in outs.values() if x.space]
    count = len(shapes) + extra_sems
    shapes += list(scratch.values())
    shapes.append(pltpu.SemaphoreType.DMA((count,)))

    def kernel(*refs):
        refs = list(refs)
        k = Kernel(refs.pop())
        arrays_in, arrays_out = [{n: refs.pop(0) for n in names} for names in (ins, outs)]
        for held, kinds in ((arrays_in, ins), (arrays_out, outs)):
            for n, x in kinds.items():
                held[n] = Array(k, held[n], refs.pop(0) if x.space else held[n])
        k.i = types.SimpleNamespace(**arrays_in)
        k.o = types.SimpleNamespace(**arrays_out)
        k.s = types.SimpleNamespace(**{n: refs.pop(0) for n in scratch})
        body(z, k)
        k.finish()

    in_hbm = pl.BlockSpec(memory_space=pltpu.HBM)
    in_vmem = pl.BlockSpec(memory_space=pltpu.VMEM)
    order_in, order_out = list(ins), list(outs)
    results = pl.pallas_call(
        kernel,
        out_shape=[pltpu.HBM(x.x, F32) for x in outs.values()],
        in_specs=[in_vmem if isinstance(x, Here) else in_hbm for x in ins.values()],
        out_specs=[in_hbm] * len(outs),
        scratch_shapes=shapes,
        input_output_aliases={order_in.index(a): order_out.index(b) for a, b in (alias or {}).items()},
        compiler_params=pltpu.CompilerParams(vmem_limit_bytes=VMEM_LIMIT),
        cost_estimate=pl.CostEstimate(
            flops=int(micros * 1e9), transcendentals=int(micros * 1e6), bytes_accessed=int(micros * 3e6)
        ),
    )(*[x.x if isinstance(x, Here) else pltpu.with_memory_space_constraint(x.x, pltpu.HBM) for x in ins.values()])
    return types.SimpleNamespace(**dict(zip(order_out, results)))


def side_of(n):
    tile = lax.axis_index("tiles")
    odd = tile % 2
    side = 1 - odd if n == 0 else odd
    there = jnp.where(side == 0, tile > 0, tile < lax.axis_size("tiles") - 1)
    return side, jnp.where(there, 1.0, 0.0)


def pack_kernel(z, k):
    small = k.i.class_n, k.i.storage, k.i.area, k.i.release, k.i.link
    load(*small)
    rows, cls_rows = k.s.rows, k.s.cls_rows
    copies = []
    for side, row in enumerate((0, z.R - 1)):
        for m in range(z.M):
            copies.append(k.copy(k.i.depth.h.at[m, pl.ds(row, 1)], rows.at[side, pl.ds(m, 1)]))
        copies.append(k.copy(k.i.bed.h.at[pl.ds(row, 1)], rows.at[side, pl.ds(z.M, 1)]))
        copies.append(k.copy(k.i.cls.h.at[pl.ds(row, 1)], cls_rows.at[side]))
    wait(*small)
    payload = k.o.payload.v
    payload[0] = jnp.zeros((z.BR, LANES), F32)
    payload[0, : z.M, : z.LD] = k.i.storage.v[...]
    for n, x in enumerate((k.i.area, k.i.release, k.i.link)):
        payload[0, z.M + n : z.M + n + 1, : z.LD] = x.v[...].astype(F32)
    for n in range(1, z.NT):
        payload[n] = payload[0]
    k.o.payload.send()
    wide = inv_table(z, k.i.class_n.v, z.PR)
    for copy in copies:
        copy.wait()
    ids = k.s.ids
    for n, out in enumerate((k.o.pack0, k.o.pack1)):
        side, _ = side_of(n)
        for g in range(z.PR):
            at = slice(g * SEG, (g + 1) * SEG)
            for m in range(z.M + 1):
                out.v[m, g : g + 1, :] = rows[side, m : m + 1, at]
            ids[g : g + 1, :] = cls_rows[side, :, at]
        for half in range(0, SEG, LANES):
            at = slice(half, half + LANES)
            out.v[z.M + 1, :, at] = look_up(wide, ids[:, at])
        out.send()


def inv_table(z, class_n, rows):
    lane = lane_ids((rows, LANES))
    names = jnp.ones((rows, LANES), F32)
    for n in range(z.classes):
        names = jnp.where(lane == n, class_n[n], names)
    return flow_rate * 0.5 / names


def look_up(table, ids):
    return jnp.take_along_axis(table, ids, axis=1, mode="promise_in_bounds")


def widen(z, ref, index=(), left=True, right=True):
    rows = slice(None)
    if left:
        ref[index + (rows, slice(0, LANES))] = pltpu.roll(ref[index + (rows, slice(LANES, 2 * LANES))], LANES - 1, 1)
    if right:
        ref[index + (rows, slice(z.W + LANES, z.W + 2 * LANES))] = pltpu.roll(
            ref[index + (rows, slice(z.W, z.W + LANES))], 1, 1
        )


def flow_blocks(z, water, bed, inv, rain, out, edges, done, ready=None):
    size = min(BLOCK, z.W)
    segs = size // SEG
    row = row_ids((z.R, size))
    bottom = row == z.R - 1
    top = row == 0

    def block(j, _):
        base = j * size if ready else pl.multiple_of(j * size, size)
        wide = pl.ds(base, size + 2 * LANES)
        at = pl.ds(base, size)
        b, v = bed[:, wide], inv[:, wide]
        for m in range(z.M):
            w = water[m, :, wide]
            s = b + w
            q = mobility(w, v)
            s_right = pltpu.roll(s, size + 2 * LANES - 1, 1)
            q_right = pltpu.roll(q, size + 2 * LANES - 1, 1)
            f = ((q + q_right) * (s - s_right))[:, : size + LANES]
            net = pltpu.roll(f, 1, 1)[:, LANES:] - f[:, LANES:]
            s = s[:, LANES : size + LANES]
            q = q[:, LANES : size + LANES]
            flow = (q + pltpu.roll(q, z.R - 1, 0)) * (s - pltpu.roll(s, z.R - 1, 0))
            flow = jnp.where(bottom, 0.0, flow)
            above = jnp.where(top, 0.0, pltpu.roll(flow, 1, 0))
            wet = w[:, LANES : size + LANES] + (net + (above - flow)) + rain[m, :, at]
            out[m, :, at] = wet
            for i in range(segs):
                part = slice(i * SEG, (i + 1) * SEG)
                edges[0, m, pl.ds(j * segs + i, 1), :] = wet[:1, part]
                edges[1, m, pl.ds(j * segs + i, 1), :] = wet[z.R - 1 :, part]
        done(j, at)
        return 0

    if ready:
        for j in range(z.W // size):
            ready(j)
            block(j, 0)
    else:
        lax.fori_loop(0, z.W // size, block, 0)


def send_blocks(z, k, source, target):
    size = min(BLOCK, z.W)
    first = k.count
    k.count += z.W // size

    def copy(j):
        at = pl.ds(pl.multiple_of(j * size, size), size)
        return pltpu.make_async_copy(source.at[:, :, at], target.at[:, :, at], k.sems.at[first + j])

    for j in range(z.W // size):
        k.stores.append(copy(j))
    return lambda j, at: copy(j).start()


def contact_places(z, seg):
    for c in range(z.C):
        owner, place = divmod(c, z.CAP)
        s = seg[0, owner, place]
        yield c, s // z.PR, pl.multiple_of((s % z.PR) * SEG, SEG)


def gather_contacts(z, seg, water, out):
    for c, r, at in contact_places(z, seg):
        for m in range(z.M):
            out[m * z.C + c : m * z.C + c + 1, :] = water[m, pl.ds(r, 1), pl.ds(at, SEG)]


def scatter_contacts(z, seg, values, water, shift):
    for c, r, at in contact_places(z, seg):
        for m in range(z.M):
            water[m, pl.ds(r, 1), pl.ds(at + shift, SEG)] = values[m * z.C + c : m * z.C + c + 1, :]


def set_edges(z, edges, water, shift):
    for side, row in enumerate((0, z.R - 1)):
        for m in range(z.M):
            for g in range(z.PR):
                at = slice(g * SEG + shift, (g + 1) * SEG + shift)
                water[m, row : row + 1, at] = edges[side, m, g : g + 1, :]


def first_kernel(z, k):
    size = min(BLOCK, z.W)
    parts = z.W // size
    small = k.i.class_n, k.i.seg, k.i.lake, k.i.slot
    load(*small)
    inv, bed, water, cls, rain = k.s.inv, k.s.bed, k.s.water, k.s.cls, k.s.rain
    coming = []
    for p in range(parts):
        at, inner = pl.ds(p * size, size), pl.ds(p * size + LANES, size)
        coming.append([
            k.copy(k.i.cls.h.at[:, at], cls.at[:, at]),
            k.copy(k.i.bed.h.at[:, at], bed.at[:, inner]),
            k.copy(k.i.depth.h.at[:, :, at], water.at[:, :, inner]),
            k.copy(k.i.rain.h.at[:, :, at], rain.at[:, :, at]),
        ])
    wait(*small)
    table = inv_table(z, k.i.class_n.v, z.R)
    one_hots(z, k)
    send(k.o.near, k.o.near_edges)

    def prepare(p):
        for copy in coming[p]:
            copy.wait()

        def look(i, _):
            at = pl.multiple_of(p * size + i * LANES, LANES)
            inv[:, pl.ds(at + LANES, LANES)] = look_up(table, cls[:, pl.ds(at, LANES)])
            return 0

        lax.fori_loop(0, size // LANES, look, 0, unroll=16)
        sides = dict(left=p == 0, right=p == parts - 1)
        widen(z, inv, **sides)
        widen(z, bed, **sides)
        for m in range(z.M):
            widen(z, water, (m,), **sides)
        at, inner = pl.ds(p * size, size), pl.ds(p * size + LANES, size)
        k.stores.append(k.copy(inv.at[:, inner], k.o.inv.h.at[:, at]))

    def ready(j):
        if j == 0:
            prepare(0)
        if j + 1 < parts:
            prepare(j + 1)

    done = send_blocks(z, k, k.s.out, k.o.wet.h)
    flow_blocks(z, water, bed, inv, rain, k.s.out, k.o.edges.v, done, ready)
    k.o.edges.send()
    gather_contacts(z, k.i.seg.v, k.s.out, k.o.wet_c.v)
    for c, r, at in contact_places(z, k.i.seg.v):
        k.o.bed_c.v[c : c + 1, :] = bed[pl.ds(r, 1), pl.ds(at + LANES, SEG)]
    send(k.o.wet_c, k.o.bed_c)


def one_hots(z, k):
    lane = lane_ids((1, LANES))
    contact = row_ids((z.C, LANES))
    place_g = row_ids((z.PR, LANES))
    inside = jnp.full((z.C, 1), z.LK, F32)
    on_edge = [jnp.full((z.PR, 1), z.LK, F32) for _ in range(2)]
    firsts = (0, (z.R - 1) * z.PR)
    for tile in range(z.CT):
        segs = jnp.full((1, LANES), -1, I32)
        slots = jnp.full((1, LANES), z.LK, I32)
        for c in range(tile * LANES, min(z.C, (tile + 1) * LANES)):
            owner, place = divmod(c, z.CAP)
            lake_id = k.i.lake.v[0, owner, place]
            found = jnp.where(lake_id >= 0, k.i.slot.v[jnp.maximum(lake_id, 0)], z.LK)
            segs = jnp.where(lane == c - tile * LANES, k.i.seg.v[0, owner, place], segs)
            slots = jnp.where(lane == c - tile * LANES, found, slots)
        more = (slots - z.LK).astype(F32)
        central = (segs >= z.PR) & (segs < firsts[1])
        mine = lane_ids((z.C, LANES)) + tile * LANES == contact
        inside += jnp.sum(jnp.where(mine & central, more, 0.0), axis=1, keepdims=True)
        for side in range(2):
            here = place_g + firsts[side] == segs
            on_edge[side] += jnp.sum(jnp.where(here, more, 0.0), axis=1, keepdims=True)
    for j in range(z.LT):
        k.o.near.v[j] = jnp.where(inside == (lane_ids((z.C, LANES)) + j * LANES).astype(F32), 1.0, 0.0)
        for side in range(2):
            ids = (lane_ids((z.PR, LANES)) + j * LANES).astype(F32)
            k.o.near_edges.v[side * z.LT + j] = jnp.where(on_edge[side] == ids, 1.0, 0.0)


def flow_kernel(z, k):
    size = min(BLOCK, z.W)
    parts = z.W // size
    inv, bed, water, rain = k.s.inv, k.s.bed, k.s.water, k.s.rain
    load(k.i.seg, k.i.water_c)
    whole = k.copy(k.i.wet.h, water.at[:, :, pl.ds(LANES, z.W)])
    k.i.edges.load()
    coming = []
    for p in range(parts):
        at, inner = pl.ds(p * size, size), pl.ds(p * size + LANES, size)
        coming.append([
            k.copy(k.i.bed.h.at[:, at], bed.at[:, inner]),
            k.copy(k.i.inv.h.at[:, at], inv.at[:, inner]),
            k.copy(k.i.rain.h.at[:, :, at], rain.at[:, :, at]),
        ])
    wait(k.i.seg, k.i.water_c)
    whole.wait()
    scatter_contacts(z, k.i.seg.v, k.i.water_c.v, water, LANES)
    k.i.edges.wait()
    set_edges(z, k.i.edges.v, water, LANES)
    for m in range(z.M):
        widen(z, water, (m,))

    def prepare(p):
        for copy in coming[p]:
            copy.wait()
        sides = dict(left=p == 0, right=p == parts - 1)
        widen(z, inv, **sides)
        widen(z, bed, **sides)

    def ready(j):
        if j == 0:
            prepare(0)
        if j + 1 < parts:
            prepare(j + 1)

    done = send_blocks(z, k, k.s.out, k.o.next.h)
    flow_blocks(z, water, bed, inv, rain, k.s.out, k.o.edges.v, done, ready)
    k.o.edges.send()
    gather_contacts(z, k.i.seg.v, k.s.out, k.o.wet_c.v)
    k.o.wet_c.send()


def last_kernel(z, k):
    load(k.i.wet, k.i.seg, k.i.water_c, k.i.edges)
    wait(k.i.wet, k.i.seg, k.i.water_c, k.i.edges)
    scatter_contacts(z, k.i.seg.v, k.i.water_c.v, k.i.wet.v, 0)
    set_edges(z, k.i.edges.v, k.i.wet.v, 0)
    k.stores.append(k.copy(k.i.wet.v, k.o.depth.h))


def pick(z, near, table, m):
    total = near[0] * table[m * z.LT : m * z.LT + 1, :]
    for j in range(1, z.LT):
        total += near[j] * table[m * z.LT + j : m * z.LT + j + 1, :]
    return jnp.sum(total, axis=1, keepdims=True)


def shift_slots(x, count):
    rows, lanes = divmod(count, LANES)
    size = x.shape[0]
    turned = pltpu.roll(x, lanes, 1) if lanes else x
    low = pltpu.roll(turned, rows % size, 0) if rows % size else turned
    if not lanes:
        return low
    high = pltpu.roll(turned, (rows + 1) % size, 0)
    return jnp.where(lane_ids(x.shape) < lanes, high, low)


def laps(z):
    count = z.LD
    while count < z.LK:
        yield count
        count *= 2


def cascade(z, consts, entering):
    for lap, count in enumerate(laps(z)):
        entering = entering + consts[3 + lap] * shift_slots(entering, count)
    return entering


def slot_ids(z):
    shape = (z.SR, LANES)
    return (row_ids(shape) % z.LT) * LANES + lane_ids(shape)


def levels_of(z, pool, area):
    return jnp.where(slot_ids(z) == z.LK, FAR, pool / area)


def lay_out(z, got, pool, consts):
    pool[...] = jnp.zeros_like(pool)
    consts[...] = jnp.zeros_like(consts)
    consts[0] = jnp.ones((z.SR, LANES), F32)
    for t in range(z.NT):
        done = 0
        while done < z.LD:
            j, at = divmod(t * z.LD + done, LANES)
            n = min(z.LD - done, LANES - at)
            for m in range(z.M):
                r = m * z.LT + j
                pool[r : r + 1, at : at + n] = got[t, m : m + 1, done : done + n]
                for i in range(3):
                    consts[i, r : r + 1, at : at + n] = got[t, z.M + i : z.M + i + 1, done : done + n]
            done += n
    consts[2] = jnp.where(slot_ids(z) >= z.LD, consts[2], 0.0)
    factor = consts[1] * consts[2]
    for lap, count in enumerate(laps(z)):
        consts[3 + lap] = factor
        factor = factor * shift_slots(factor, count)


def cross_edges(z, k, own, other, rows):
    for n in range(2):
        side, flag = side_of(n)
        own_bed, own_inv, other_bed, other_inv = rows(side, n)
        for m in range(z.M):
            a, b = own(side, n, m), other(n, m)
            flow = (mobility(a, own_inv) + mobility(b, other_inv)) * ((other_bed + b) - (own_bed + a))
            k.i.edges.v[side, m] += flow * flag


def contact_step(z, k, level, bed_rows):
    rows = [[jnp.zeros((SUBLANES, LANES), F32) for _ in range(z.LT)] for _ in range(z.M)]

    def take(near, m, w, bed):
        taken = taken_of(w, bed + w, pick(z, near, level, m))
        sums = jnp.sum(taken, axis=1, keepdims=True) * (1.0 / SEG)
        for j in range(z.LT):
            part = near[j] * sums
            for r in range(0, part.shape[0], SUBLANES):
                rows[m][j] += part[r : r + SUBLANES]
        return w - taken

    for side in range(2):
        near = k.i.near_edges.v.at[pl.ds(side * z.LT, z.LT)]
        for m in range(z.M):
            k.o.edges.v[side, m] = take(near, m, k.i.edges.v[side, m], bed_rows(side))
    bed = k.i.bed_c.v[...]
    for m in range(z.M):
        at = slice(m * z.C, (m + 1) * z.C)
        k.o.water_c.v[at, :] = take(k.i.near.v, m, k.i.wet_c.v[at, :], bed)
    found = [jnp.sum(rows[m][j], axis=0, keepdims=True) for m in range(z.M) for j in range(z.LT)]
    if z.SR > len(found):
        found.append(jnp.zeros((z.SR - len(found), LANES), F32))
    return jnp.concatenate(found, axis=0)


def send_edges(z, k, exchange):
    k.o.edges.send()
    if exchange:
        for n, out in enumerate((k.o.edge0, k.o.edge1)):
            side, _ = side_of(n)
            k.stores.append(k.copy(k.o.edges.v.at[side], out.h))


def open_kernel(z, k):
    load(k.i.edges, k.i.own0, k.i.own1, k.i.near, k.i.near_edges, k.i.wet_c, k.i.bed_c)
    own, other, pack = (k.i.own0, k.i.own1), (k.i.from0, k.i.from1), k.o.pack.v
    wait(k.i.edges, k.i.own0, k.i.own1)
    for n in range(2):
        side, _ = side_of(n)
        pack[side, :2] = own[n].v[z.M : z.M + 2]
        pack[side, 2:] = other[n].v[z.M : z.M + 2]
    k.o.pack.send()
    cross_edges(
        z, k,
        lambda side, n, m: own[n].v[m],
        lambda n, m: other[n].v[m],
        lambda side, n: [pack[side, i] for i in range(4)],
    )
    pool, consts = k.s.pool, k.o.consts.v
    lay_out(z, k.i.got.v, pool, consts)
    k.o.consts.send()
    k.o.state.v[0] = pool[...]
    k.o.state.v[1] = jnp.zeros((z.SR, LANES), F32)
    k.o.state.send()
    k.s.level[...] = levels_of(z, pool[...], consts[0])
    wait(k.i.near, k.i.near_edges, k.i.wet_c, k.i.bed_c)
    sums = contact_step(z, k, k.s.level, lambda side: pack[side, 0])
    for n in range(z.NT):
        k.o.payload.v[n] = sums
    send(k.o.payload, k.o.water_c)
    send_edges(z, k, True)


def step_reservoirs(z, consts, pool, total, lateral):
    area, release, link = consts[0], consts[1], consts[2]
    released = cascade(z, consts, release * (pool + lateral))
    pool = pool + lateral + link * shift_slots(released, z.LD) - released
    return pool, total + released


def sum_members(z, x):
    total = x
    for m in range(1, z.M):
        total = total + pltpu.roll(x, z.SR - m * z.LT, 0)
    return jnp.where(row_ids(x.shape) < z.LT, total, 0.0)


def contact_kernel(z, k, last):
    load(k.i.state, k.i.consts, k.i.own, k.i.pack, k.i.edges, k.i.near_edges, k.i.near, k.i.wet_c, k.i.bed_c)
    wait(k.i.state, k.i.consts)
    got, consts = k.i.got.v, k.i.consts.v
    lateral = got[0]
    for t in range(1, z.NT):
        lateral += got[t]
    pool, total = step_reservoirs(z, consts, k.i.state.v[0], k.i.state.v[1], lateral)
    k.o.state.v[0] = pool
    k.o.state.v[1] = total
    k.o.state.send()
    k.s.level[...] = levels_of(z, pool, consts[0])
    wait(k.i.own, k.i.pack, k.i.edges)
    other, pack = (k.i.from0, k.i.from1), k.i.pack.v
    cross_edges(
        z, k,
        lambda side, n, m: k.i.own.v[side, m],
        lambda n, m: other[n].v[m],
        lambda side, n: [pack[side, i] for i in range(4)],
    )
    wait(k.i.near_edges, k.i.near, k.i.wet_c, k.i.bed_c)
    sums = contact_step(z, k, k.s.level, lambda side: pack[side, 0])
    payload = k.o.payload.v
    if last:
        summed = sum_members(z, total) * (1.0 / z.NT)
        others = consts[1] * (sum_members(z, sums) + sum_members(z, pool) * (1.0 / z.NT))
        others = others + summed - consts[3] * shift_slots(summed, z.LD)
        member = lax.axis_index("ens")
        for e in range(z.E):
            block = jnp.where(member == e, sums, others)
            for t in range(z.NT):
                payload[e * z.NT + t] = block
    else:
        for t in range(z.NT):
            payload[t] = sums
    send(k.o.payload, k.o.water_c)
    send_edges(z, k, not last)


def own_slots(z, x, tile):
    begin = tile * z.LD
    at = begin % LANES
    j = begin // LANES
    out = jnp.zeros((1, LANES), F32)
    turned = pltpu.roll(x, LANES - at, 1)
    lane = lane_ids((1, LANES))
    for n in range(z.LT):
        out = jnp.where((j == n) & (lane < LANES - at), turned[n : n + 1], out)
        out = jnp.where((j + 1 == n) & (lane >= LANES - at), turned[n : n + 1], out)
    return out


def close_kernel(z, k):
    load(k.i.state, k.i.consts)
    wait(k.i.state, k.i.consts)
    tile = lax.axis_index("tiles")
    member = lax.axis_index("ens")
    got, consts = k.i.got.v, k.i.consts.v
    lateral = jnp.zeros((z.SR, LANES), F32)
    others = jnp.zeros((z.SR, LANES), F32)
    for e in range(z.E):
        part = got[e * z.NT]
        for t in range(1, z.NT):
            part += got[e * z.NT + t]
        lateral = jnp.where(member == e, part, lateral)
        others = others + jnp.where(member == e, 0.0, part)
    pool, total = step_reservoirs(z, consts, k.i.state.v[0], k.i.state.v[1], lateral)
    for m in range(z.M):
        at = slice(m * z.LT, (m + 1) * z.LT)
        k.o.storage.v[m : m + 1, :] = own_slots(z, pool[at], tile)[:, : z.LD]
    mean = (sum_members(z, total) + cascade(z, consts, others)) * (1.0 / (z.M * z.E))
    k.o.outflow.v[...] = own_slots(z, mean[: z.LT], tile)[:, : z.LD]
    send(k.o.storage, k.o.outflow)


def shards(
    depth, bed, rain, rough_class, class_n, contact_seg, contact_lake, lake_slot, storage, area, release, upstream_link
):
    z = types.SimpleNamespace()
    z.M, z.R, z.W = depth.shape
    z.NT = lax.axis_size("tiles")
    z.E = lax.axis_size("ens")
    z.LD = storage.shape[1]
    z.LK = z.NT * z.LD
    z.CAP = contact_seg.shape[2]
    z.C = contact_seg.shape[1] * z.CAP
    z.CT = -(-z.C // LANES)
    z.PR = z.W // SEG
    z.classes = class_n.shape[0]
    z.LT = z.LK // LANES + 1
    z.SR = up_to(z.M * z.LT, SUBLANES)
    z.BR = up_to(z.M + 3, SUBLANES)
    levels = len(list(laps(z)))
    blocks = z.W // min(BLOCK, z.W)
    tile_shape = (z.M, z.R, z.W)
    edge_shape = (z.M, z.PR, SEG)
    pack_shape = (z.M + 2, z.PR, SEG)
    near_shape = (z.LT, z.C, LANES)
    state_shape = (2, z.SR, LANES)
    const_shape = (3 + levels, z.SR, LANES)
    contact_shape = (z.M * z.C, SEG)
    wide_tile = pltpu.VMEM((z.M, z.R, z.W + 2 * LANES), F32)
    wide_rows = pltpu.VMEM((z.R, z.W + 2 * LANES), F32)
    plain_tile = pltpu.VMEM(tile_shape, F32)
    partner = [i ^ 1 for i in range(z.NT)], [((i + 1) ^ 1) - 1 for i in range(z.NT)]
    pairs = [[(i, j) for i, j in enumerate(js) if 0 <= j < z.NT] for js in partner]

    def share(x, axes):
        return lax.all_to_all(x, axes, 0, 0, tiled=True)

    def swap(x, y):
        return lax.ppermute(x, "tiles", pairs[0]), lax.ppermute(y, "tiles", pairs[1])

    edges_shape = (2,) + edge_shape
    level_buffer = pltpu.VMEM((z.SR, LANES), F32)
    opened = staged_call(
        pack_kernel, z,
        dict(depth=Raw(depth), bed=Raw(bed), cls=Raw(rough_class), class_n=Scalars(class_n), storage=storage,
             area=area.reshape(1, -1), release=release.reshape(1, -1), link=upstream_link.reshape(1, -1)),
        dict(pack0=pack_shape, pack1=pack_shape, payload=(z.NT, z.BR, LANES)),
        dict(rows=pltpu.VMEM((2, z.M + 1, z.W), F32), cls_rows=pltpu.VMEM((2, 1, z.W), I32), ids=pltpu.VMEM((z.PR, SEG), I32)),
        extra_sems=2 * (z.M + 2),
    )
    got = share(opened.payload, "tiles")
    from0, from1 = swap(opened.pack0, opened.pack1)
    flow = staged_call(
        first_kernel, z,
        dict(depth=Raw(depth), bed=Raw(bed), rain=Raw(rain), cls=Raw(rough_class), class_n=Scalars(class_n),
             seg=Scalars(contact_seg), lake=Scalars(contact_lake), slot=Scalars(lake_slot)),
        dict(wet=Raw(tile_shape), inv=Raw((z.R, z.W)), edges=edges_shape, wet_c=contact_shape, bed_c=(z.C, SEG),
             near=near_shape, near_edges=(2 * z.LT, z.PR, LANES)),
        dict(water=wide_tile, bed=wide_rows, inv=wide_rows, rain=plain_tile, out=plain_tile, cls=pltpu.VMEM((z.R, z.W), I32)),
        extra_sems=6 * blocks,
    )
    inv, bed_c, near, near_edges = flow.inv, flow.bed_c, flow.near, flow.near_edges
    wet, wet_c, edges = flow.wet, flow.wet_c, flow.edges

    step_out = dict(edges=edges_shape, water_c=contact_shape, state=state_shape)
    exchange_out = dict(edge0=Raw(edge_shape), edge1=Raw(edge_shape))
    now = staged_call(
        open_kernel, z,
        dict(got=Here(got), from0=Here(from0), from1=Here(from1), own0=opened.pack0, own1=opened.pack1, edges=edges,
             near=near, near_edges=near_edges, wet_c=wet_c, bed_c=bed_c),
        dict(payload=(z.NT, z.SR, LANES), pack=(2, 4, z.PR, SEG), consts=const_shape, **step_out, **exchange_out),
        dict(pool=level_buffer, level=level_buffer),
        extra_sems=2,
    )
    consts, pack = now.consts, now.pack
    for step in range(1, STEPS):
        got = share(now.payload, "tiles")
        from0, from1 = swap(now.edge0, now.edge1)
        last = step == STEPS - 1
        flow = staged_call(
            flow_kernel, z,
            dict(wet=Raw(wet), seg=Scalars(contact_seg), water_c=now.water_c, edges=now.edges, bed=Raw(bed), inv=Raw(inv),
                 rain=Raw(rain)),
            dict(next=Raw(tile_shape), wet_c=contact_shape, edges=edges_shape),
            dict(water=wide_tile, bed=wide_rows, inv=wide_rows, rain=plain_tile, out=plain_tile),
            extra_sems=1 + 4 * blocks,
        )
        wet, wet_c, edges = flow.next, flow.wet_c, flow.edges
        now = staged_call(
            functools.partial(contact_kernel, last=last), z,
            dict(got=Here(got), from0=Here(from0), from1=Here(from1), own=now.edges, edges=edges, state=now.state,
                 consts=consts, pack=pack, near=near, near_edges=near_edges, wet_c=wet_c, bed_c=bed_c),
            dict(payload=((z.E if last else 1) * z.NT, z.SR, LANES), **step_out, **({} if last else exchange_out)),
            dict(level=level_buffer),
            extra_sems=2,
        )
    got = share(now.payload, ("ens", "tiles"))
    new_depth = staged_call(
        last_kernel, z,
        dict(wet=wet, seg=Scalars(contact_seg), water_c=now.water_c, edges=now.edges),
        dict(depth=Raw(tile_shape)),
        extra_sems=1,
    ).depth
    closed = staged_call(
        close_kernel, z,
        dict(got=Here(got), state=now.state, consts=consts),
        dict(storage=(z.M, z.LD), outflow=(1, z.LD)),
    )
    return new_depth, closed.storage, closed.outflow.reshape(-1)


def solution(mesh):
    return jax.shard_map(
        shards,
        mesh=mesh,
        in_specs=(
            P("ens", "tiles", None),
            P("tiles", None),
            P("ens", "tiles", None),
            P("tiles", None),
            P(),
            P("tiles", None, None),
            P("tiles", None, None),
            P(),
            P("ens", "tiles"),
            P("tiles"),
            P("tiles"),
            P("tiles"),
        ),
        out_specs=(P("ens", "tiles", None), P("ens", "tiles"), P("tiles")),
        check_vma=False,
    )
```

profile of v0, /device:TPU:0, one launch (start us, length us, event | category | flops | bytes accessed | tf_op | source)
XLA Modules:
  0.0 98.5 jit_solution(6066998913651345325)
XLA Ops:
  0.6 2.2 %shard_map.140 = (f32[4,64,256]{2,1,0:T(8,128)}, f32[4,64,256]{2,1,0:T(8,128)}, f32[8,8,128]{2,1,0:T(8,128)}) custom-call(f32[2,16,16384]{2,1,0:T(8,128)} %refs_0_.3, f32[16,16384]{1,0:T(8,128)} %refs_4_.9, s32[16,16384]{1,0:T(8,128)} %refs_2_.3, f32[16]{0:T(128)} %refs_3_.3, f32[2,40]{1,0:T(2,128)} %refs_4_.6, f32[1,40]{1,0:T(1,128)} %bitcast.4, ...), custom_call_target="tpu_custom_call" | custom-call | flops 60000002048 | bytes 180000000 | tf_op jit(solution)/shard_map/pallas_call | solution.py:136
  2.9 7.3 %all-to-all-start = ((f32[8,8,128]{2,1,0:T(8,128)}), f32[8,8,128]{2,1,0:T(8,128)S(1)}, u32[]{:S(2)}, u32[]{:S(2)}) async-start(f32[8,8,128]{2,1,0:T(8,128)} %get-tuple-element.49), calls=%async_computation | async-start | bytes 65536 | tf_op jit(solution)/shard_map/all_to_all | solution.py:692
  10.2 2.0 %collective-permute-start = (f32[4,64,256]{2,1,0:T(8,128)}, f32[4,64,256]{2,1,0:T(8,128)S(1)}, u32[]{:S(2)}, u32[]{:S(2)}) collective-permute-start(f32[4,64,256]{2,1,0:T(8,128)} %get-tuple-element.50.refs_3_), channel_id=1, source_target_pairs={{0,4},{4,0},{8,12},{12,8},{16,20},{20,16},{24,28},{28,24},{1,5},{5... | collective-permute-start | bytes 786440 | tf_op jit(solution)/shard_map/ppermute | solution.py:695
  12.2 0.7 collective-permute-start.1
  12.8 6.9 %shard_map.139 = (f32[2,16,16384]{2,1,0:T(8,128)}, f32[16,16384]{1,0:T(8,128)}, f32[2,2,64,256]{3,2,1,0:T(8,128)}, f32[128,256]{1,0:T(8,128)}, f32[64,256]{1,0:T...) custom-call(f32[2,16,16384]{2,1,0:T(8,128)} %refs_0_.3, f32[16,16384]{1,0:T(8,128)} %refs_4_.9, ...), custom_call_target="tpu_custom_call" | custom-call | flops 60000002048 | bytes 180000000 | tf_op jit(solution)/shard_map/pallas_call | solution.py:136
  19.7 0.0 all-to-all-done.refs_0_
  19.7 3.6 %collective-permute-done.refs_1_ = f32[4,64,256]{2,1,0:T(8,128)S(1)} collective-permute-done((f32[4,64,256]{2,1,0:T(8,128)}, f32[4,64,256]{2,1,0:T(8,128)S(1)}, u32[]{:S(2)}, u32[]{:S(2)}) %collective-permute-start) | collective-permute-done | bytes 262176 | tf_op jit(solution)/shard_map/ppermute | solution.py:695
  23.3 0.0 collective-permute-done.1.refs_2_
  23.3 2.7 %shard_map.141 = (f32[8,8,128]{2,1,0:T(8,128)}, f32[2,4,64,256]{3,2,1,0:T(8,128)}, f32[6,8,128]{2,1,0:T(8,128)}, f32[2,2,64,256]{3,2,1,0:T(8,128)}, f32[128,256]...) custom-call(f32[8,8,128]{2,1,0:T(8,128)S(1)} %all-to-all-done.refs_0_, ...), custom_call_target="tpu_custom_call" | custom-call | flops 60000002048 | bytes 180000000 | tf_op jit(solution)/shard_map/pallas_call | solution.py:136
  26.1 5.4 %all-to-all-start.1 = ((f32[8,8,128]{2,1,0:T(8,128)}), f32[8,8,128]{2,1,0:T(8,128)S(1)}, u32[]{:S(2)}, u32[]{:S(2)}) async-start(f32[8,8,128]{2,1,0:T(8,128)} %get-tuple-element.61), calls=%async_computation.1 | async-start | bytes 65536 | tf_op jit(solution)/shard_map/all_to_all | solution.py:692
  31.5 2.0 %collective-permute-start.2 = (f32[2,64,256]{2,1,0:T(8,128)}, f32[2,64,256]{2,1,0:T(8,128)S(1)}, u32[]{:S(2)}, u32[]{:S(2)}) collective-permute-start(f32[2,64,256]{2,1,0:T(8,128)} %get-tuple-element.62), channel_id=1, source_target_pairs={{0,4},{4,0},{8,12},{12,8},{16,20},{20,16},{24,28},{28,24},{1,5},{5... | collective-permute-start | bytes 393224 | tf_op jit(solution)/shard_map/ppermute | solution.py:695
  33.5 0.7 collective-permute-start.3
  34.2 6.4 %shard_map.142 = (f32[2,16,16384]{2,1,0:T(8,128)}, f32[128,256]{1,0:T(8,128)}, f32[2,2,64,256]{3,2,1,0:T(8,128)}) custom-call(f32[2,16,16384]{2,1,0:T(8,128)} %get-tuple-element.48.refs_0_, s32[1,8,8]{2,1,0:T(8,128)} %refs_1_.11, f32[128,256]{1,0:T(8,128)} %get-tuple-element.57.refs_2_, f32[2,2,64,256]{3,2,1,0:T(8,128)} %get-tuple-element.58.refs_3_, ...), custom_call_target="tpu_custom_call" | custom-call | flops 60000002048 | bytes 180000000 | tf_op jit(solution)/shard_map/pallas_call | solution.py:136
  40.6 0.0 all-to-all-done.1.refs_0_
  40.6 0.0 collective-permute-done.2.refs_1_
  40.6 0.0 collective-permute-done.3.refs_2_
  40.6 2.7 %shard_map.143 = (f32[8,8,128]{2,1,0:T(8,128)}, f32[2,2,64,256]{3,2,1,0:T(8,128)}, f32[128,256]{1,0:T(8,128)}, f32[2,8,128]{2,1,0:T(8,128)}, f32[2,64,256]{2,1,0:T(8,128)}, /*index=5*/f32[2,64,256]{2,1,0:T(8,128)}) custom-call(f32[8,8,128]{2,1,0:T(8,128)S(1)} %all-to-all-done.1.refs_0_, f32[2,64,256]{2,1,0:T(8,128)S(1)} %collective-permute-done.2.refs_1_, ...), custom_call_target="tpu_custom_call" | custom-call | flops 60000002048 | bytes 180000000 | tf_op jit(solution)/shard_map/pallas_call | solution.py:136
  43.3 7.3 %all-to-all-start.2 = ((f32[8,8,128]{2,1,0:T(8,128)}), f32[8,8,128]{2,1,0:T(8,128)S(1)}, u32[]{:S(2)}, u32[]{:S(2)}) async-start(f32[8,8,128]{2,1,0:T(8,128)} %get-tuple-element.72), calls=%async_computation.2 | async-start | bytes 65536 | tf_op jit(solution)/shard_map/all_to_all | solution.py:692
  50.6 2.0 %collective-permute-start.4 = (f32[2,64,256]{2,1,0:T(8,128)}, f32[2,64,256]{2,1,0:T(8,128)S(1)}, u32[]{:S(2)}, u32[]{:S(2)}) collective-permute-start(f32[2,64,256]{2,1,0:T(8,128)} %get-tuple-element.73), channel_id=1, source_target_pairs={{0,4},{4,0},{8,12},{12,8},{16,20},{20,16},{24,28},{28,24},{1,5},{5... | collective-permute-start | bytes 393224 | tf_op jit(solution)/shard_map/ppermute | solution.py:695
  52.6 0.8 collective-permute-start.5
  53.4 6.4 %shard_map.144 = (f32[2,16,16384]{2,1,0:T(8,128)}, f32[128,256]{1,0:T(8,128)}, f32[2,2,64,256]{3,2,1,0:T(8,128)}) custom-call(f32[2,16,16384]{2,1,0:T(8,128)} %get-tuple-element.60.refs_0_, s32[1,8,8]{2,1,0:T(8,128)} %refs_1_.11, f32[128,256]{1,0:T(8,128)} %get-tuple-element.69.refs_2_, f32[2,2,64,256]{3,2,1,0:T(8,128)} %get-tuple-element.70.refs_3_, ...), custom_call_target="tpu_custom_call" | custom-call | flops 60000002048 | bytes 180000000 | tf_op jit(solution)/shard_map/pallas_call | solution.py:136
  59.8 0.0 all-to-all-done.2.refs_0_
  59.8 0.0 collective-permute-done.4.refs_1_
  59.8 0.0 collective-permute-done.5.refs_2_
  59.8 2.7 %shard_map.145 = (f32[8,8,128]{2,1,0:T(8,128)}, f32[2,2,64,256]{3,2,1,0:T(8,128)}, f32[128,256]{1,0:T(8,128)}, f32[2,8,128]{2,1,0:T(8,128)}, f32[2,64,256]{2,1,0:T(8,128)}, /*index=5*/f32[2,64,256]{2,1,0:T(8,128)}) custom-call(f32[8,8,128]{2,1,0:T(8,128)S(1)} %all-to-all-done.2.refs_0_, f32[2,64,256]{2,1,0:T(8,128)S(1)} %collective-permute-done.4.refs_1_, ...), custom_call_target="tpu_custom_call" | custom-call | flops 60000002048 | bytes 180000000 | tf_op jit(solution)/shard_map/pallas_call | solution.py:136
  62.6 7.3 %all-to-all-start.3 = ((f32[8,8,128]{2,1,0:T(8,128)}), f32[8,8,128]{2,1,0:T(8,128)S(1)}, u32[]{:S(2)}, u32[]{:S(2)}) async-start(f32[8,8,128]{2,1,0:T(8,128)} %get-tuple-element.81), calls=%async_computation.3 | async-start | bytes 65536 | tf_op jit(solution)/shard_map/all_to_all | solution.py:692
  69.8 2.0 %collective-permute-start.6 = (f32[2,64,256]{2,1,0:T(8,128)}, f32[2,64,256]{2,1,0:T(8,128)S(1)}, u32[]{:S(2)}, u32[]{:S(2)}) collective-permute-start(f32[2,64,256]{2,1,0:T(8,128)} %get-tuple-element.82), channel_id=1, source_target_pairs={{0,4},{4,0},{8,12},{12,8},{16,20},{20,16},{24,28},{28,24},{1,5},{5... | collective-permute-start | bytes 393224 | tf_op jit(solution)/shard_map/ppermute | solution.py:695
  71.8 0.7 collective-permute-start.7
  72.5 6.4 %shard_map.146 = (f32[2,16,16384]{2,1,0:T(8,128)}, f32[128,256]{1,0:T(8,128)}, f32[2,2,64,256]{3,2,1,0:T(8,128)}) custom-call(f32[2,16,16384]{2,1,0:T(8,128)} %get-tuple-element.71.refs_0_, s32[1,8,8]{2,1,0:T(8,128)} %refs_1_.11, f32[128,256]{1,0:T(8,128)} %get-tuple-element.78.refs_2_, f32[2,2,64,256]{3,2,1,0:T(8,128)} %get-tuple-element.79.refs_3_, ...), custom_call_target="tpu_custom_call" | custom-call | flops 60000002048 | bytes 180000000 | tf_op jit(solution)/shard_map/pallas_call | solution.py:136
  78.9 0.0 all-to-all-done.3.refs_0_
  78.9 0.0 collective-permute-done.6.refs_1_
  78.9 0.0 collective-permute-done.7.refs_2_
  78.9 2.6 %shard_map.147 = (f32[32,8,128]{2,1,0:T(8,128)}, f32[2,2,64,256]{3,2,1,0:T(8,128)}, f32[128,256]{1,0:T(8,128)}, f32[2,8,128]{2,1,0:T(8,128)}) custom-call(f32[8,8,128]{2,1,0:T(8,128)S(1)} %all-to-all-done.3.refs_0_, f32[2,64,256]{2,1,0:T(8,128)S(1)} %collective-permute-done.6.refs_1_, f32[2,64,256]{2,1,0:T(8,128)S(1)} %collective-permute-done.7.refs_2_, ...), custom_call_target="tpu_custom_call" | custom-call | flops 60000002048 | bytes 180000000 | tf_op jit(solution)/shard_map/pallas_call | solution.py:136
  81.6 7.3 %all-to-all-start.4 = ((f32[32,8,128]{2,1,0:T(8,128)}), f32[32,8,128]{2,1,0:T(8,128)S(1)}, u32[]{:S(2)}, u32[]{:S(2)}) async-start(f32[32,8,128]{2,1,0:T(8,128)} %get-tuple-element.89), calls=%async_computation.4 | async-start | bytes 262144 | tf_op jit(solution)/shard_map/all_to_all | solution.py:692
  88.9 3.6 %shard_map.148 = f32[2,16,16384]{2,1,0:T(8,128)} custom-call(f32[2,16,16384]{2,1,0:T(8,128)} %get-tuple-element.80.refs_0_, s32[1,8,8]{2,1,0:T(8,128)} %refs_1_.11, f32[128,256]{1,0:T(8,128)} %get-tuple-element.87.refs_2_, f32[2,2,64,256]{3,2,1,0:T(8,128)} %get-tuple-element.88.refs_3_), custom_call_target="tpu_custom_call" | custom-call | flops 60000002048 | bytes 180000000 | tf_op jit(solution)/shard_map/pallas_call | solution.py:136
  92.5 4.1 %all-to-all-done.4.refs_0_ = f32[32,8,128]{2,1,0:T(8,128)S(1)} async-done(((f32[32,8,128]{2,1,0:T(8,128)}), f32[32,8,128]{2,1,0:T(8,128)S(1)}, u32[]{:S(2)}, u32[]{:S(2)}) %all-to-all-start.4) | async-done | bytes 131104 | tf_op jit(solution)/shard_map/all_to_all | solution.py:692
  96.6 1.7 %shard_map.149 = (f32[2,40]{1,0:T(2,128)}, f32[1,40]{1,0:T(1,128)}) custom-call(f32[32,8,128]{2,1,0:T(8,128)S(1)} %all-to-all-done.4.refs_0_, f32[2,8,128]{2,1,0:T(8,128)} %get-tuple-element.90.refs_1_, f32[6,8,128]{2,1,0:T(8,128)} %get-tuple-element.66.refs_6_.refs_2_), custom_call_target="tpu_custom_call" | custom-call | flops 60000002048 | bytes 180000000 | tf_op jit(solution)/shard_map/pallas_call | solution.py:136
Async XLA Ops:
  2.9 16.8 %all-to-all-start = ((f32[8,8,128]{2,1,0:T(8,128)}), f32[8,8,128]{2,1,0:T(8,128)S(1)}, u32[]{:S(2)}, u32[]{:S(2)}) async-start(f32[8,8,128]{2,1,0:T(8,128)} %get-tuple-element.49), calls=%async_computation | async-start | bytes 65536 | tf_op jit(solution)/shard_map/all_to_all | solution.py:692
  10.2 13.2 %collective-permute-start = (f32[4,64,256]{2,1,0:T(8,128)}, f32[4,64,256]{2,1,0:T(8,128)S(1)}, u32[]{:S(2)}, u32[]{:S(2)}) collective-permute-start(f32[4,64,256]{2,1,0:T(8,128)} %get-tuple-element.50.refs_3_), channel_id=1, source_target_pairs={{0,4},{4,0},{8,12},{12,8},{16,20},{20,16},{24,28},{28,24},{1,5},{5... | collective-permute-start | bytes 786440 | tf_op jit(solution)/shard_map/ppermute | solution.py:695
  12.2 11.2 %collective-permute-start.1 = (f32[4,64,256]{2,1,0:T(8,128)}, f32[4,64,256]{2,1,0:T(8,128)S(1)}, u32[]{:S(2)}, u32[]{:S(2)}) collective-permute-start(f32[4,64,256]{2,1,0:T(8,128)} %get-tuple-element.51.refs_4_), channel_id=1, source_target_pairs={{4,8},{8,4},{12,16},{16,12},{20,24},{24,20},{5,9},{9,5},{13,17},{1... | collective-permute-start | bytes 786440 | tf_op jit(solution)/shard_map/ppermute | solution.py:695
  26.1 14.5 %all-to-all-start.1 = ((f32[8,8,128]{2,1,0:T(8,128)}), f32[8,8,128]{2,1,0:T(8,128)S(1)}, u32[]{:S(2)}, u32[]{:S(2)}) async-start(f32[8,8,128]{2,1,0:T(8,128)} %get-tuple-element.61), calls=%async_computation.1 | async-start | bytes 65536 | tf_op jit(solution)/shard_map/all_to_all | solution.py:692
  31.5 9.1 %collective-permute-start.2 = (f32[2,64,256]{2,1,0:T(8,128)}, f32[2,64,256]{2,1,0:T(8,128)S(1)}, u32[]{:S(2)}, u32[]{:S(2)}) collective-permute-start(f32[2,64,256]{2,1,0:T(8,128)} %get-tuple-element.62), channel_id=1, source_target_pairs={{0,4},{4,0},{8,12},{12,8},{16,20},{20,16},{24,28},{28,24},{1,5},{5... | collective-permute-start | bytes 393224 | tf_op jit(solution)/shard_map/ppermute | solution.py:695
  33.5 7.1 %collective-permute-start.3 = (f32[2,64,256]{2,1,0:T(8,128)}, f32[2,64,256]{2,1,0:T(8,128)S(1)}, u32[]{:S(2)}, u32[]{:S(2)}) collective-permute-start(f32[2,64,256]{2,1,0:T(8,128)} %get-tuple-element.63), channel_id=1, source_target_pairs={{4,8},{8,4},{12,16},{16,12},{20,24},{24,20},{5,9},{9,5},{13,17},{1... | collective-permute-start | bytes 393224 | tf_op jit(solution)/shard_map/ppermute | solution.py:695
  43.3 16.5 %all-to-all-start.2 = ((f32[8,8,128]{2,1,0:T(8,128)}), f32[8,8,128]{2,1,0:T(8,128)S(1)}, u32[]{:S(2)}, u32[]{:S(2)}) async-start(f32[8,8,128]{2,1,0:T(8,128)} %get-tuple-element.72), calls=%async_computation.2 | async-start | bytes 65536 | tf_op jit(solution)/shard_map/all_to_all | solution.py:692
  50.6 9.3 %collective-permute-start.4 = (f32[2,64,256]{2,1,0:T(8,128)}, f32[2,64,256]{2,1,0:T(8,128)S(1)}, u32[]{:S(2)}, u32[]{:S(2)}) collective-permute-start(f32[2,64,256]{2,1,0:T(8,128)} %get-tuple-element.73), channel_id=1, source_target_pairs={{0,4},{4,0},{8,12},{12,8},{16,20},{20,16},{24,28},{28,24},{1,5},{5... | collective-permute-start | bytes 393224 | tf_op jit(solution)/shard_map/ppermute | solution.py:695
  52.6 7.2 %collective-permute-start.5 = (f32[2,64,256]{2,1,0:T(8,128)}, f32[2,64,256]{2,1,0:T(8,128)S(1)}, u32[]{:S(2)}, u32[]{:S(2)}) collective-permute-start(f32[2,64,256]{2,1,0:T(8,128)} %get-tuple-element.74), channel_id=1, source_target_pairs={{4,8},{8,4},{12,16},{16,12},{20,24},{24,20},{5,9},{9,5},{13,17},{1... | collective-permute-start | bytes 393224 | tf_op jit(solution)/shard_map/ppermute | solution.py:695
  62.6 16.3 %all-to-all-start.3 = ((f32[8,8,128]{2,1,0:T(8,128)}), f32[8,8,128]{2,1,0:T(8,128)S(1)}, u32[]{:S(2)}, u32[]{:S(2)}) async-start(f32[8,8,128]{2,1,0:T(8,128)} %get-tuple-element.81), calls=%async_computation.3 | async-start | bytes 65536 | tf_op jit(solution)/shard_map/all_to_all | solution.py:692
  69.8 9.1 %collective-permute-start.6 = (f32[2,64,256]{2,1,0:T(8,128)}, f32[2,64,256]{2,1,0:T(8,128)S(1)}, u32[]{:S(2)}, u32[]{:S(2)}) collective-permute-start(f32[2,64,256]{2,1,0:T(8,128)} %get-tuple-element.82), channel_id=1, source_target_pairs={{0,4},{4,0},{8,12},{12,8},{16,20},{20,16},{24,28},{28,24},{1,5},{5... | collective-permute-start | bytes 393224 | tf_op jit(solution)/shard_map/ppermute | solution.py:695
  71.8 7.1 %collective-permute-start.7 = (f32[2,64,256]{2,1,0:T(8,128)}, f32[2,64,256]{2,1,0:T(8,128)S(1)}, u32[]{:S(2)}, u32[]{:S(2)}) collective-permute-start(f32[2,64,256]{2,1,0:T(8,128)} %get-tuple-element.83), channel_id=1, source_target_pairs={{4,8},{8,4},{12,16},{16,12},{20,24},{24,20},{5,9},{9,5},{13,17},{1... | collective-permute-start | bytes 393224 | tf_op jit(solution)/shard_map/ppermute | solution.py:695
  81.6 15.0 %all-to-all-start.4 = ((f32[32,8,128]{2,1,0:T(8,128)}), f32[32,8,128]{2,1,0:T(8,128)S(1)}, u32[]{:S(2)}, u32[]{:S(2)}) async-start(f32[32,8,128]{2,1,0:T(8,128)} %get-tuple-element.89), calls=%async_computation.4 | async-start | bytes 262144 | tf_op jit(solution)/shard_map/all_to_all | solution.py:692
where the time goes:
time: 99.4 us; the launch traced here: 98.5 us
  starting transfers between devices  45.4 us (46%)
  Pallas kernels  44.4 us (45%)
  waiting for transfers between devices  7.73 us (8%)
  between operations  1 us (1%)
    pallas_call x11, Pallas kernels, staged_call(): pl.pallas_call(kernel, out_shape=[pltpu.HBM(x.x, F32) for x in outs.value...  44.4 us
    all_to_all x5, starting transfers between devices, share(): return lax.all_to_all(x, axes, 0, 0, tiled=True)  34.5 us
    ppermute x4, starting transfers between devices, swap(): lax.ppermute(x, 'tiles', pairs[0])  8.08 us
    all_to_all x5, waiting for transfers between devices, share(): return lax.all_to_all(x, axes, 0, 0, tiled=True)  4.12 us
    ppermute x4, waiting for transfers between devices, swap(): lax.ppermute(x, 'tiles', pairs[0])  3.6 us
    ppermute x4, starting transfers between devices, swap(): lax.ppermute(y, 'tiles', pairs[1])  2.82 us
  transfers between devices with their start and end apart: 13, of which 2 were waited for; matrix products, arithmetic and copies ran while one was open for 0% of the time, Pallas kernels for 30%

commit v1 on v0

--- a/solution.py
+++ b/solution.py
@@ -68,6 +68,10 @@
         copy.start()
         return copy
 
+    def pass_on(self):
+        for source, target in self.passed:
+            self.stores.append(self.copy(source, target))
+
     def finish(self):
         for copy in self.stores:
             copy.wait()
@@ -91,8 +95,8 @@
 class Staged:
     space = pltpu.VMEM
 
-    def __init__(self, x):
-        self.x = x
+    def __init__(self, x, free=False):
+        self.x, self.free = x, free
 
 
 class Scalars(Staged):
@@ -105,12 +109,21 @@
 
 class Here(Staged):
     space = None
+
+
+class Passed(Here):
+    pass
 
 
 def staged_call(body, z, ins, outs, scratch=None, alias=None, extra_sems=0, micros=60):
     scratch = scratch or {}
     ins = {n: x if isinstance(x, Staged) else Staged(x) for n, x in ins.items()}
-    outs = {n: x if isinstance(x, Raw) else Staged(x) for n, x in outs.items()}
+    outs = {n: x if isinstance(x, Staged) else Staged(x) for n, x in outs.items()}
+    passed = [n for n, x in ins.items() if isinstance(x, Passed)]
+    outs.update({n: Here(ins[n].x.shape) for n in passed})
+    extra_sems += len(passed)
+    here_in = [isinstance(x, Here) and not isinstance(x, Passed) for x in ins.values()]
+    here_out = [isinstance(x, Here) for x in outs.values()]
     shapes = [x.space(x.x.shape, x.x.dtype) for x in ins.values() if x.space]
     shapes += [x.space(x.x, F32) for x in outs.values() if x.space]
     count = len(shapes) + extra_sems
@@ -127,6 +140,7 @@
         k.i = types.SimpleNamespace(**arrays_in)
         k.o = types.SimpleNamespace(**arrays_out)
         k.s = types.SimpleNamespace(**{n: refs.pop(0) for n in scratch})
+        k.passed = [(arrays_in[n].h, arrays_out[n].h) for n in passed]
         body(z, k)
         k.finish()
 
@@ -135,16 +149,19 @@
     order_in, order_out = list(ins), list(outs)
     results = pl.pallas_call(
         kernel,
-        out_shape=[pltpu.HBM(x.x, F32) for x in outs.values()],
-        in_specs=[in_vmem if isinstance(x, Here) else in_hbm for x in ins.values()],
-        out_specs=[in_hbm] * len(outs),
+        out_shape=[(pltpu.VMEM if here else pltpu.HBM)(x.x, F32) for x, here in zip(outs.values(), here_out)],
+        in_specs=[in_vmem if here else in_hbm for here in here_in],
+        out_specs=[in_vmem if here else in_hbm for here in here_out],
         scratch_shapes=shapes,
         input_output_aliases={order_in.index(a): order_out.index(b) for a, b in (alias or {}).items()},
         compiler_params=pltpu.CompilerParams(vmem_limit_bytes=VMEM_LIMIT),
         cost_estimate=pl.CostEstimate(
             flops=int(micros * 1e9), transcendentals=int(micros * 1e6), bytes_accessed=int(micros * 3e6)
         ),
-    )(*[x.x if isinstance(x, Here) else pltpu.with_memory_space_constraint(x.x, pltpu.HBM) for x in ins.values()])
+    )(*[
+        pltpu.with_memory_space_constraint(x.x, pltpu.VMEM if here else pltpu.HBM) if not (here and x.free) else x.x
+        for x, here in zip(ins.values(), here_in)
+    ])
     return types.SimpleNamespace(**dict(zip(order_out, results)))
 
 
@@ -157,8 +174,7 @@
 
 
 def pack_kernel(z, k):
-    small = k.i.class_n, k.i.storage, k.i.area, k.i.release, k.i.link
-    load(*small)
+    k.i.class_n.load()
     rows, cls_rows = k.s.rows, k.s.cls_rows
     copies = []
     for side, row in enumerate((0, z.R - 1)):
@@ -166,15 +182,9 @@
             copies.append(k.copy(k.i.depth.h.at[m, pl.ds(row, 1)], rows.at[side, pl.ds(m, 1)]))
         copies.append(k.copy(k.i.bed.h.at[pl.ds(row, 1)], rows.at[side, pl.ds(z.M, 1)]))
         copies.append(k.copy(k.i.cls.h.at[pl.ds(row, 1)], cls_rows.at[side]))
-    wait(*small)
-    payload = k.o.payload.v
-    payload[0] = jnp.zeros((z.BR, LANES), F32)
-    payload[0, : z.M, : z.LD] = k.i.storage.v[...]
-    for n, x in enumerate((k.i.area, k.i.release, k.i.link)):
-        payload[0, z.M + n : z.M + n + 1, : z.LD] = x.v[...].astype(F32)
-    for n in range(1, z.NT):
-        payload[n] = payload[0]
-    k.o.payload.send()
+    k.i.class_n.wait()
+    k.o.table.v[...] = inv_table(z, k.i.class_n.v, z.R)
+    k.o.table.send()
     wide = inv_table(z, k.i.class_n.v, z.PR)
     for copy in copies:
         copy.wait()
@@ -297,57 +307,36 @@
                 water[m, row : row + 1, at] = edges[side, m, g : g + 1, :]
 
 
-def first_kernel(z, k):
+def prepare_kernel(z, k):
     size = min(BLOCK, z.W)
     parts = z.W // size
-    small = k.i.class_n, k.i.seg, k.i.lake, k.i.slot
+    small = k.i.seg, k.i.lake, k.i.slot, k.i.storage, k.i.area, k.i.release, k.i.link, k.i.table
     load(*small)
-    inv, bed, water, cls, rain = k.s.inv, k.s.bed, k.s.water, k.s.cls, k.s.rain
-    coming = []
+    cls, inv = k.s.cls, k.s.inv
+    columns = [pl.ds(p * size, size) for p in range(parts)]
+    coming = [k.copy(k.i.cls.h.at[:, at], cls.at[:, at]) for at in columns]
+    wait(*small)
+    payload = k.o.payload.v
+    payload[0] = jnp.zeros((z.BR, LANES), F32)
+    payload[0, : z.M, : z.LD] = k.i.storage.v[...]
+    for n, x in enumerate((k.i.area, k.i.release, k.i.link)):
+        payload[0, z.M + n : z.M + n + 1, : z.LD] = x.v[...].astype(F32)
+    for n in range(1, z.NT):
+        payload[n] = payload[0]
+    k.o.payload.send()
+    table = k.i.table.v[...]
     for p in range(parts):
-        at, inner = pl.ds(p * size, size), pl.ds(p * size + LANES, size)
-        coming.append([
-            k.copy(k.i.cls.h.at[:, at], cls.at[:, at]),
-            k.copy(k.i.bed.h.at[:, at], bed.at[:, inner]),
-            k.copy(k.i.depth.h.at[:, :, at], water.at[:, :, inner]),
-            k.copy(k.i.rain.h.at[:, :, at], rain.at[:, :, at]),
-        ])
-    wait(*small)
-    table = inv_table(z, k.i.class_n.v, z.R)
+        coming[p].wait()
+
+        def look(i, _):
+            at = pl.ds(pl.multiple_of(p * size + i * LANES, LANES), LANES)
+            inv[:, at] = look_up(table, cls[:, at])
+            return 0
+
+        lax.fori_loop(0, size // LANES, look, 0, unroll=16)
+        k.stores.append(k.copy(inv.at[:, columns[p]], k.o.inv.h.at[:, columns[p]]))
     one_hots(z, k)
     send(k.o.near, k.o.near_edges)
-
-    def prepare(p):
-        for copy in coming[p]:
-            copy.wait()
-
-        def look(i, _):
-            at = pl.multiple_of(p * size + i * LANES, LANES)
-            inv[:, pl.ds(at + LANES, LANES)] = look_up(table, cls[:, pl.ds(at, LANES)])
-            return 0
-
-        lax.fori_loop(0, size // LANES, look, 0, unroll=16)
-        sides = dict(left=p == 0, right=p == parts - 1)
-        widen(z, inv, **sides)
-        widen(z, bed, **sides)
-        for m in range(z.M):
-            widen(z, water, (m,), **sides)
-        at, inner = pl.ds(p * size, size), pl.ds(p * size + LANES, size)
-        k.stores.append(k.copy(inv.at[:, inner], k.o.inv.h.at[:, at]))
-
-    def ready(j):
-        if j == 0:
-            prepare(0)
-        if j + 1 < parts:
-            prepare(j + 1)
-
-    done = send_blocks(z, k, k.s.out, k.o.wet.h)
-    flow_blocks(z, water, bed, inv, rain, k.s.out, k.o.edges.v, done, ready)
-    k.o.edges.send()
-    gather_contacts(z, k.i.seg.v, k.s.out, k.o.wet_c.v)
-    for c, r, at in contact_places(z, k.i.seg.v):
-        k.o.bed_c.v[c : c + 1, :] = bed[pl.ds(r, 1), pl.ds(at + LANES, SEG)]
-    send(k.o.wet_c, k.o.bed_c)
 
 
 def one_hots(z, k):
@@ -380,28 +369,33 @@
             k.o.near_edges.v[side * z.LT + j] = jnp.where(on_edge[side] == ids, 1.0, 0.0)
 
 
-def flow_kernel(z, k):
+def flow_kernel(z, k, first):
     size = min(BLOCK, z.W)
     parts = z.W // size
     inv, bed, water, rain = k.s.inv, k.s.bed, k.s.water, k.s.rain
-    load(k.i.seg, k.i.water_c)
-    whole = k.copy(k.i.wet.h, water.at[:, :, pl.ds(LANES, z.W)])
-    k.i.edges.load()
+    k.i.seg.load()
+    columns = [(pl.ds(p * size, size), pl.ds(p * size + LANES, size)) for p in range(parts)]
+    if not first:
+        k.i.water_c.load()
+        whole = k.copy(k.i.wet.h, water.at[:, :, pl.ds(LANES, z.W)])
+        k.i.edges.load()
     coming = []
-    for p in range(parts):
-        at, inner = pl.ds(p * size, size), pl.ds(p * size + LANES, size)
+    for at, inner in columns:
         coming.append([
             k.copy(k.i.bed.h.at[:, at], bed.at[:, inner]),
             k.copy(k.i.inv.h.at[:, at], inv.at[:, inner]),
             k.copy(k.i.rain.h.at[:, :, at], rain.at[:, :, at]),
         ])
-    wait(k.i.seg, k.i.water_c)
-    whole.wait()
-    scatter_contacts(z, k.i.seg.v, k.i.water_c.v, water, LANES)
-    k.i.edges.wait()
-    set_edges(z, k.i.edges.v, water, LANES)
-    for m in range(z.M):
-        widen(z, water, (m,))
+        if first:
+            coming[-1].append(k.copy(k.i.wet.h.at[:, :, at], water.at[:, :, inner]))
+    k.pass_on()
+    k.i.seg.wait()
+    if not first:
+        k.i.water_c.wait()
+        whole.wait()
+        scatter_contacts(z, k.i.seg.v, k.i.water_c.v, water, LANES)
+        k.i.edges.wait()
+        set_edges(z, k.i.edges.v, water, LANES)
 
     def prepare(p):
         for copy in coming[p]:
@@ -409,6 +403,8 @@
         sides = dict(left=p == 0, right=p == parts - 1)
         widen(z, inv, **sides)
         widen(z, bed, **sides)
+        for m in range(z.M):
+            widen(z, water, (m,), **sides)
 
     def ready(j):
         if j == 0:
@@ -418,13 +414,17 @@
 
     done = send_blocks(z, k, k.s.out, k.o.next.h)
     flow_blocks(z, water, bed, inv, rain, k.s.out, k.o.edges.v, done, ready)
-    k.o.edges.send()
     gather_contacts(z, k.i.seg.v, k.s.out, k.o.wet_c.v)
-    k.o.wet_c.send()
+    if first:
+        for c, r, at in contact_places(z, k.i.seg.v):
+            k.o.bed_c.v[c : c + 1, :] = bed[pl.ds(r, 1), pl.ds(at + LANES, SEG)]
+            k.s.bed_c[c : c + 1, :] = bed[pl.ds(r, 1), pl.ds(at + LANES, SEG)]
+        k.stores.append(k.copy(k.s.bed_c, k.o.bed_kept.h))
 
 
 def last_kernel(z, k):
     load(k.i.wet, k.i.seg, k.i.water_c, k.i.edges)
+    k.pass_on()
     wait(k.i.wet, k.i.seg, k.i.water_c, k.i.edges)
     scatter_contacts(z, k.i.seg.v, k.i.water_c.v, k.i.wet.v, 0)
     set_edges(z, k.i.edges.v, k.i.wet.v, 0)
@@ -538,9 +538,7 @@
 
 
 def open_kernel(z, k):
-    load(k.i.edges, k.i.own0, k.i.own1, k.i.near, k.i.near_edges, k.i.wet_c, k.i.bed_c)
     own, other, pack = (k.i.own0, k.i.own1), (k.i.from0, k.i.from1), k.o.pack.v
-    wait(k.i.edges, k.i.own0, k.i.own1)
     for n in range(2):
         side, _ = side_of(n)
         pack[side, :2] = own[n].v[z.M : z.M + 2]
@@ -559,7 +557,6 @@
     k.o.state.v[1] = jnp.zeros((z.SR, LANES), F32)
     k.o.state.send()
     k.s.level[...] = levels_of(z, pool[...], consts[0])
-    wait(k.i.near, k.i.near_edges, k.i.wet_c, k.i.bed_c)
     sums = contact_step(z, k, k.s.level, lambda side: pack[side, 0])
     for n in range(z.NT):
         k.o.payload.v[n] = sums
@@ -582,8 +579,6 @@
 
 
 def contact_kernel(z, k, last):
-    load(k.i.state, k.i.consts, k.i.own, k.i.pack, k.i.edges, k.i.near_edges, k.i.near, k.i.wet_c, k.i.bed_c)
-    wait(k.i.state, k.i.consts)
     got, consts = k.i.got.v, k.i.consts.v
     lateral = got[0]
     for t in range(1, z.NT):
@@ -593,7 +588,6 @@
     k.o.state.v[1] = total
     k.o.state.send()
     k.s.level[...] = levels_of(z, pool, consts[0])
-    wait(k.i.own, k.i.pack, k.i.edges)
     other, pack = (k.i.from0, k.i.from1), k.i.pack.v
     cross_edges(
         z, k,
@@ -601,7 +595,6 @@
         lambda n, m: other[n].v[m],
         lambda side, n: [pack[side, i] for i in range(4)],
     )
-    wait(k.i.near_edges, k.i.near, k.i.wet_c, k.i.bed_c)
     sums = contact_step(z, k, k.s.level, lambda side: pack[side, 0])
     payload = k.o.payload.v
     if last:
@@ -634,8 +627,6 @@
 
 
 def close_kernel(z, k):
-    load(k.i.state, k.i.consts)
-    wait(k.i.state, k.i.consts)
     tile = lax.axis_index("tiles")
     member = lax.axis_index("ens")
     got, consts = k.i.got.v, k.i.consts.v
@@ -698,32 +689,42 @@
     level_buffer = pltpu.VMEM((z.SR, LANES), F32)
     opened = staged_call(
         pack_kernel, z,
-        dict(depth=Raw(depth), bed=Raw(bed), cls=Raw(rough_class), class_n=Scalars(class_n), storage=storage,
-             area=area.reshape(1, -1), release=release.reshape(1, -1), link=upstream_link.reshape(1, -1)),
-        dict(pack0=pack_shape, pack1=pack_shape, payload=(z.NT, z.BR, LANES)),
+        dict(depth=Raw(depth), bed=Raw(bed), cls=Raw(rough_class), class_n=Scalars(class_n)),
+        dict(pack0=pack_shape, pack1=pack_shape, table=(z.R, LANES)),
         dict(rows=pltpu.VMEM((2, z.M + 1, z.W), F32), cls_rows=pltpu.VMEM((2, 1, z.W), I32), ids=pltpu.VMEM((z.PR, SEG), I32)),
         extra_sems=2 * (z.M + 2),
     )
-    got = share(opened.payload, "tiles")
     from0, from1 = swap(opened.pack0, opened.pack1)
+    kept = staged_call(
+        prepare_kernel, z,
+        dict(cls=Raw(rough_class), table=opened.table, seg=Scalars(contact_seg), lake=Scalars(contact_lake),
+             slot=Scalars(lake_slot), storage=storage, area=area.reshape(1, -1), release=release.reshape(1, -1),
+             link=upstream_link.reshape(1, -1)),
+        dict(payload=(z.NT, z.BR, LANES), inv=Raw((z.R, z.W)), near=near_shape, near_edges=(2 * z.LT, z.PR, LANES)),
+        dict(cls=pltpu.VMEM((z.R, z.W), I32), inv=pltpu.VMEM((z.R, z.W), F32)),
+        extra_sems=2 * blocks,
+    )
+    got = share(kept.payload, "tiles")
+    inv, near, near_edges = kept.inv, kept.near, kept.near_edges
+    flow_scratch = dict(water=wide_tile, bed=wide_rows, inv=wide_rows, rain=plain_tile, out=plain_tile)
+    flow_out = dict(next=Raw(tile_shape), wet_c=Here(contact_shape), edges=Here(edges_shape))
     flow = staged_call(
-        first_kernel, z,
-        dict(depth=Raw(depth), bed=Raw(bed), rain=Raw(rain), cls=Raw(rough_class), class_n=Scalars(class_n),
-             seg=Scalars(contact_seg), lake=Scalars(contact_lake), slot=Scalars(lake_slot)),
-        dict(wet=Raw(tile_shape), inv=Raw((z.R, z.W)), edges=edges_shape, wet_c=contact_shape, bed_c=(z.C, SEG),
-             near=near_shape, near_edges=(2 * z.LT, z.PR, LANES)),
-        dict(water=wide_tile, bed=wide_rows, inv=wide_rows, rain=plain_tile, out=plain_tile, cls=pltpu.VMEM((z.R, z.W), I32)),
-        extra_sems=6 * blocks,
-    )
-    inv, bed_c, near, near_edges = flow.inv, flow.bed_c, flow.near, flow.near_edges
-    wet, wet_c, edges = flow.wet, flow.wet_c, flow.edges
+        functools.partial(flow_kernel, first=True), z,
+        dict(wet=Raw(depth), seg=Scalars(contact_seg), bed=Raw(bed), inv=Raw(inv), rain=Raw(rain), near=Passed(near),
+             near_edges=Passed(near_edges), own0=Passed(opened.pack0), own1=Passed(opened.pack1)),
+        dict(bed_c=Here((z.C, SEG)), bed_kept=Raw((z.C, SEG)), **flow_out),
+        dict(bed_c=pltpu.VMEM((z.C, SEG), F32), **flow_scratch),
+        extra_sems=5 * blocks + 1,
+    )
+    bed_kept = flow.bed_kept
 
     step_out = dict(edges=edges_shape, water_c=contact_shape, state=state_shape)
     exchange_out = dict(edge0=Raw(edge_shape), edge1=Raw(edge_shape))
     now = staged_call(
         open_kernel, z,
-        dict(got=Here(got), from0=Here(from0), from1=Here(from1), own0=opened.pack0, own1=opened.pack1, edges=edges,
-             near=near, near_edges=near_edges, wet_c=wet_c, bed_c=bed_c),
+        dict(got=Here(got, free=True), from0=Here(from0, free=True), from1=Here(from1, free=True), own0=Here(flow.own0),
+             own1=Here(flow.own1), edges=Here(flow.edges), near=Here(flow.near), near_edges=Here(flow.near_edges),
+             wet_c=Here(flow.wet_c), bed_c=Here(flow.bed_c)),
         dict(payload=(z.NT, z.SR, LANES), pack=(2, 4, z.PR, SEG), consts=const_shape, **step_out, **exchange_out),
         dict(pool=level_buffer, level=level_buffer),
         extra_sems=2,
@@ -734,35 +735,37 @@
         from0, from1 = swap(now.edge0, now.edge1)
         last = step == STEPS - 1
         flow = staged_call(
-            flow_kernel, z,
-            dict(wet=Raw(wet), seg=Scalars(contact_seg), water_c=now.water_c, edges=now.edges, bed=Raw(bed), inv=Raw(inv),
-                 rain=Raw(rain)),
-            dict(next=Raw(tile_shape), wet_c=contact_shape, edges=edges_shape),
-            dict(water=wide_tile, bed=wide_rows, inv=wide_rows, rain=plain_tile, out=plain_tile),
+            functools.partial(flow_kernel, first=False), z,
+            dict(wet=Raw(flow.next), seg=Scalars(contact_seg), water_c=now.water_c, edges=now.edges, bed=Raw(bed),
+                 inv=Raw(inv), rain=Raw(rain), state=Passed(now.state), consts=Passed(consts), near=Passed(near),
+                 near_edges=Passed(near_edges), pack=Passed(pack), own=Passed(now.edges), bed_c=Passed(bed_kept)),
+            flow_out,
+            flow_scratch,
             extra_sems=1 + 4 * blocks,
         )
-        wet, wet_c, edges = flow.next, flow.wet_c, flow.edges
         now = staged_call(
             functools.partial(contact_kernel, last=last), z,
-            dict(got=Here(got), from0=Here(from0), from1=Here(from1), own=now.edges, edges=edges, state=now.state,
-                 consts=consts, pack=pack, near=near, near_edges=near_edges, wet_c=wet_c, bed_c=bed_c),
+            dict(got=Here(got, free=True), from0=Here(from0, free=True), from1=Here(from1, free=True), own=Here(flow.own),
+                 edges=Here(flow.edges), state=Here(flow.state), consts=Here(flow.consts), pack=Here(flow.pack),
+                 near=Here(flow.near), near_edges=Here(flow.near_edges), wet_c=Here(flow.wet_c), bed_c=Here(flow.bed_c)),
             dict(payload=((z.E if last else 1) * z.NT, z.SR, LANES), **step_out, **({} if last else exchange_out)),
             dict(level=level_buffer),
             extra_sems=2,
         )
     got = share(now.payload, ("ens", "tiles"))
-    new_depth = staged_call(
+    done = staged_call(
         last_kernel, z,
-        dict(wet=wet, seg=Scalars(contact_seg), water_c=now.water_c, edges=now.edges),
+        dict(wet=flow.next, seg=Scalars(contact_seg), water_c=now.water_c, edges=now.edges, state=Passed(now.state),
+             consts=Passed(consts)),
         dict(depth=Raw(tile_shape)),
         extra_sems=1,
-    ).depth
+    )
     closed = staged_call(
         close_kernel, z,
-        dict(got=Here(got), state=now.state, consts=consts),
+        dict(got=Here(got, free=True), state=Here(done.state), consts=Here(done.consts)),
         dict(storage=(z.M, z.LD), outflow=(1, z.LD)),
     )
-    return new_depth, closed.storage, closed.outflow.reshape(-1)
+    return done.depth, closed.storage, closed.outflow.reshape(-1)
 
 
 def solution(mesh):

time: 99.4 us -> 93.5 us (0.941)
  Pallas kernels: 44.4 us -> 40.4 us
  waiting for transfers between devices: 7.73 us -> 5.32 us
    pallas_call x11 -> x12, Pallas kernels: 44.4 us -> 40.4 us  [staged_call(): pl.pallas_call(kernel, out_shape=[(pltpu.VMEM if here else pltpu.HBM)(x.x...]
    ppermute x4, waiting for transfers between devices: 3.6 us -> 0.01 us  [swap(): lax.ppermute(x, 'tiles', pairs[0])]
    all_to_all x5, waiting for transfers between devices: 4.12 us -> 5.3 us  [share(): return lax.all_to_all(x, axes, 0, 0, tiled=True)]
  transfers between devices with their start and end apart: 13 -> 13, of which waited for: 2 -> 2; matrix products, arithmetic and copies ran while one was open for 0% -> 0% of each run, Pallas kernels for 30% -> 33%
where the time goes in v1:
time: 93.5 us; the launch traced here: 92.8 us
  starting transfers between devices  46 us (49%)
  Pallas kernels  40.4 us (43%)
  waiting for transfers between devices  5.32 us (6%)
  between operations  0.99 us (1%)
    pallas_call x12, Pallas kernels, staged_call(): pl.pallas_call(kernel, out_shape=[(pltpu.VMEM if here else pltpu.HBM)(x.x...  40.4 us
    all_to_all x5, starting transfers between devices, share(): return lax.all_to_all(x, axes, 0, 0, tiled=True)  34.2 us
    ppermute x4, starting transfers between devices, swap(): lax.ppermute(x, 'tiles', pairs[0])  9.07 us
    all_to_all x5, waiting for transfers between devices, share(): return lax.all_to_all(x, axes, 0, 0, tiled=True)  5.3 us
    ppermute x4, starting transfers between devices, swap(): lax.ppermute(y, 'tiles', pairs[1])  2.82 us
  transfers between devices with their start and end apart: 13, of which 2 were waited for; matrix products, arithmetic and copies ran while one was open for 0% of the time, Pallas kernels for 33%

profile of v1, /device:TPU:0, one launch (start us, length us, event | category | flops | bytes accessed | tf_op | source)
XLA Modules:
  0.0 92.8 jit_solution(6297242706274366561)
XLA Ops:
  0.6 2.2 %shard_map.139 = (f32[4,64,256]{2,1,0:T(8,128)}, f32[4,64,256]{2,1,0:T(8,128)}, f32[16,128]{1,0:T(8,128)}) custom-call(f32[2,16,16384]{2,1,0:T(8,128)} %refs_0_.5, f32[16,16384]{1,0:T(8,128)} %refs_4_.9, s32[16,16384]{1,0:T(8,128)} %refs_0_.4, f32[16]{0:T(128)} %refs_3_.2), custom_call_target="tpu_custom_call" | custom-call | flops 60000002048 | bytes 180000000 | tf_op jit(solution)/shard_map/pallas_call | solution.py:150
  2.8 3.0 %collective-permute-start = (f32[4,64,256]{2,1,0:T(8,128)}, f32[4,64,256]{2,1,0:T(8,128)S(1)}, u32[]{:S(2)}, u32[]{:S(2)}) collective-permute-start(f32[4,64,256]{2,1,0:T(8,128)} %get-tuple-element.82.refs_7_), channel_id=1, source_target_pairs={{0,4},{4,0},{8,12},{12,8},{16,20},{20,16},{24,28},{28,24},{1,5},{5... | collective-permute-start | bytes 786440 | tf_op jit(solution)/shard_map/ppermute | solution.py:686
  5.8 0.7 collective-permute-start.1
  6.5 3.4 %shard_map.140 = (f32[8,8,128]{2,1,0:T(8,128)}, f32[16,16384]{1,0:T(8,128)}, f32[3,64,128]{2,1,0:T(8,128)}, f32[6,64,128]{2,1,0:T(8,128)}) custom-call(s32[16,16384]{1,0:T(8,128)} %refs_0_.4, f32[16,128]{1,0:T(8,128)} %get-tuple-element.78.refs_1_, s32[1,8,8]{2,1,0:T(8,128)} %refs_1_.11, s32[1,8,8]{2,1,0:T(8,128)} %refs_3_.3, s32[320]{0:T(512)} %refs_4_.5, ...), custom_call_target="tpu_custom_call" | custom-call | flops 60000002048 | bytes 180000000 | tf_op jit(solution)/shard_map/pallas_call | solution.py:150
  9.9 7.6 %all-to-all-start = ((f32[8,8,128]{2,1,0:T(8,128)}), f32[8,8,128]{2,1,0:T(8,128)S(1)}, u32[]{:S(2)}, u32[]{:S(2)}) async-start(f32[8,8,128]{2,1,0:T(8,128)} %get-tuple-element.85), calls=%async_computation | async-start | bytes 65536 | tf_op jit(solution)/shard_map/all_to_all | solution.py:683
  17.5 5.5 %shard_map.141 = (f32[64,256]{1,0:T(8,128)S(1)}, f32[64,256]{1,0:T(8,128)}, f32[2,16,16384]{2,1,0:T(8,128)}, f32[128,256]{1,0:T(8,128)S(1)}, f32[2,2,64,256]{3,2...) custom-call(f32[2,16,16384]{2,1,0:T(8,128)} %refs_0_.5, ...), custom_call_target="tpu_custom_call" | custom-call | flops 60000002048 | bytes 180000000 | tf_op jit(solution)/shard_map/pallas_call | solution.py:150
  22.9 1.2 %all-to-all-done.refs_0_ = f32[8,8,128]{2,1,0:T(8,128)S(1)} async-done(((f32[8,8,128]{2,1,0:T(8,128)}), f32[8,8,128]{2,1,0:T(8,128)S(1)}, u32[]{:S(2)}, u32[]{:S(2)}) %all-to-all-start) | async-done | bytes 32800 | tf_op jit(solution)/shard_map/all_to_all | solution.py:683
  24.1 0.0 collective-permute-done.refs_1_
  24.1 0.0 collective-permute-done.1.refs_2_
  24.2 1.6 %shard_map.142 = (f32[8,8,128]{2,1,0:T(8,128)}, f32[2,4,64,256]{3,2,1,0:T(8,128)}, f32[6,8,128]{2,1,0:T(8,128)}, f32[2,2,64,256]{3,2,1,0:T(8,128)}, f32[128,256]...) custom-call(f32[8,8,128]{2,1,0:T(8,128)S(1)} %all-to-all-done.refs_0_, ...), custom_call_target="tpu_custom_call" | custom-call | flops 60000002048 | bytes 180000000 | tf_op jit(solution)/shard_map/pallas_call | solution.py:150
  25.8 4.8 %all-to-all-start.1 = ((f32[8,8,128]{2,1,0:T(8,128)}), f32[8,8,128]{2,1,0:T(8,128)S(1)}, u32[]{:S(2)}, u32[]{:S(2)}) async-start(f32[8,8,128]{2,1,0:T(8,128)} %get-tuple-element.100), calls=%async_computation.1 | async-start | bytes 65536 | tf_op jit(solution)/shard_map/all_to_all | solution.py:683
  30.6 2.0 %collective-permute-start.2 = (f32[2,64,256]{2,1,0:T(8,128)}, f32[2,64,256]{2,1,0:T(8,128)S(1)}, u32[]{:S(2)}, u32[]{:S(2)}) collective-permute-start(f32[2,64,256]{2,1,0:T(8,128)} %get-tuple-element.101), channel_id=1, source_target_pairs={{0,4},{4,0},{8,12},{12,8},{16,20},{20,16},{24,28},{28,24},{1,5},{5... | collective-permute-start | bytes 393224 | tf_op jit(solution)/shard_map/ppermute | solution.py:686
  32.6 0.7 collective-permute-start.3
  33.3 6.1 %shard_map.143 = (f32[2,16,16384]{2,1,0:T(8,128)}, f32[128,256]{1,0:T(8,128)S(1)}, f32[2,2,64,256]{3,2,1,0:T(8,128)S(1)}, f32[2,8,128]{2,1,0:T(8,128)S(1)}, f32[...) custom-call(f32[2,16,16384]{2,1,0:T(8,128)} %get-tuple-element.84.re, ...), custom_call_target="tpu_custom_call" | custom-call | flops 60000002048 | bytes 180000000 | tf_op jit(solution)/shard_map/pallas_call | solution.py:150
  39.4 0.0 all-to-all-done.1.refs_0_
  39.4 0.0 collective-permute-done.2.refs_1_
  39.4 0.0 collective-permute-done.3.refs_2_
  39.4 1.7 %shard_map.144 = (f32[8,8,128]{2,1,0:T(8,128)}, f32[2,2,64,256]{3,2,1,0:T(8,128)}, f32[128,256]{1,0:T(8,128)}, f32[2,8,128]{2,1,0:T(8,128)}, f32[2,64,256]{2,1,0:T(8,128)}, /*index=5*/f32[2,64,256]{2,1,0:T(8,128)}) custom-call(f32[8,8,128]{2,1,0:T(8,128)S(1)} %all-to-all-done.1.refs_0_, f32[2,64,256]{2,1,0:T(8,128)S(1)} %collective-permute-done.2.refs_1_, ...), custom_call_target="tpu_custom_call" | custom-call | flops 60000002048 | bytes 180000000 | tf_op jit(solution)/shard_map/pallas_call | solution.py:150
  41.1 7.2 %all-to-all-start.2 = ((f32[8,8,128]{2,1,0:T(8,128)}), f32[8,8,128]{2,1,0:T(8,128)S(1)}, u32[]{:S(2)}, u32[]{:S(2)}) async-start(f32[8,8,128]{2,1,0:T(8,128)} %get-tuple-element.116), calls=%async_computation.2 | async-start | bytes 65536 | tf_op jit(solution)/shard_map/all_to_all | solution.py:683
  48.3 2.0 %collective-permute-start.4 = (f32[2,64,256]{2,1,0:T(8,128)}, f32[2,64,256]{2,1,0:T(8,128)S(1)}, u32[]{:S(2)}, u32[]{:S(2)}) collective-permute-start(f32[2,64,256]{2,1,0:T(8,128)} %get-tuple-element.117), channel_id=1, source_target_pairs={{0,4},{4,0},{8,12},{12,8},{16,20},{20,16},{24,28},{28,24},{1,5},{5... | collective-permute-start | bytes 393224 | tf_op jit(solution)/shard_map/ppermute | solution.py:686
  50.3 0.8 collective-permute-start.5
  51.2 6.0 %shard_map.145 = (f32[2,16,16384]{2,1,0:T(8,128)}, f32[128,256]{1,0:T(8,128)S(1)}, f32[2,2,64,256]{3,2,1,0:T(8,128)S(1)}, f32[2,8,128]{2,1,0:T(8,128)S(1)}, f32[...) custom-call(f32[2,16,16384]{2,1,0:T(8,128)} %get-tuple-element.99.re, ...), custom_call_target="tpu_custom_call" | custom-call | flops 60000002048 | bytes 180000000 | tf_op jit(solution)/shard_map/pallas_call | solution.py:150
  57.2 0.0 all-to-all-done.2.refs_0_
  57.3 0.0 collective-permute-done.4.refs_1_
  57.3 0.0 collective-permute-done.5.refs_2_
  57.3 1.7 %shard_map.146 = (f32[8,8,128]{2,1,0:T(8,128)}, f32[2,2,64,256]{3,2,1,0:T(8,128)}, f32[128,256]{1,0:T(8,128)}, f32[2,8,128]{2,1,0:T(8,128)}, f32[2,64,256]{2,1,0:T(8,128)}, /*index=5*/f32[2,64,256]{2,1,0:T(8,128)}) custom-call(f32[8,8,128]{2,1,0:T(8,128)S(1)} %all-to-all-done.2.refs_0_, f32[2,64,256]{2,1,0:T(8,128)S(1)} %collective-permute-done.4.refs_1_, ...), custom_call_target="tpu_custom_call" | custom-call | flops 60000002048 | bytes 180000000 | tf_op jit(solution)/shard_map/pallas_call | solution.py:150
  59.0 7.2 %all-to-all-start.3 = ((f32[8,8,128]{2,1,0:T(8,128)}), f32[8,8,128]{2,1,0:T(8,128)S(1)}, u32[]{:S(2)}, u32[]{:S(2)}) async-start(f32[8,8,128]{2,1,0:T(8,128)} %get-tuple-element.132), calls=%async_computation.3 | async-start | bytes 65536 | tf_op jit(solution)/shard_map/all_to_all | solution.py:683
  66.2 2.0 %collective-permute-start.6 = (f32[2,64,256]{2,1,0:T(8,128)}, f32[2,64,256]{2,1,0:T(8,128)S(1)}, u32[]{:S(2)}, u32[]{:S(2)}) collective-permute-start(f32[2,64,256]{2,1,0:T(8,128)} %get-tuple-element.133), channel_id=1, source_target_pairs={{0,4},{4,0},{8,12},{12,8},{16,20},{20,16},{24,28},{28,24},{1,5},{5... | collective-permute-start | bytes 393224 | tf_op jit(solution)/shard_map/ppermute | solution.py:686
  68.2 0.7 collective-permute-start.7
  68.9 6.1 %shard_map.147 = (f32[2,16,16384]{2,1,0:T(8,128)}, f32[128,256]{1,0:T(8,128)S(1)}, f32[2,2,64,256]{3,2,1,0:T(8,128)S(1)}, f32[2,8,128]{2,1,0:T(8,128)S(1)}, f32[...) custom-call(f32[2,16,16384]{2,1,0:T(8,128)} %get-tuple-element.115.r, ...), custom_call_target="tpu_custom_call" | custom-call | flops 60000002048 | bytes 180000000 | tf_op jit(solution)/shard_map/pallas_call | solution.py:150
  75.0 0.0 all-to-all-done.3.refs_0_
  75.0 0.0 collective-permute-done.6.refs_1_
  75.0 0.0 collective-permute-done.7.refs_2_
  75.0 1.7 %shard_map.148 = (f32[32,8,128]{2,1,0:T(8,128)}, f32[2,2,64,256]{3,2,1,0:T(8,128)}, f32[128,256]{1,0:T(8,128)}, f32[2,8,128]{2,1,0:T(8,128)}) custom-call(f32[8,8,128]{2,1,0:T(8,128)S(1)} %all-to-all-done.3.refs_0_, f32[2,64,256]{2,1,0:T(8,128)S(1)} %collective-permute-done.6.refs_1_, f32[2,64,256]{2,1,0:T(8,128)S(1)} %collective-permute-done.7.refs_2_, ...), custom_call_target="tpu_custom_call" | custom-call | flops 60000002048 | bytes 180000000 | tf_op jit(solution)/shard_map/pallas_call | solution.py:150
  76.7 7.3 %all-to-all-start.4 = ((f32[32,8,128]{2,1,0:T(8,128)}), f32[32,8,128]{2,1,0:T(8,128)S(1)}, u32[]{:S(2)}, u32[]{:S(2)}) async-start(f32[32,8,128]{2,1,0:T(8,128)} %get-tuple-element.148), calls=%async_computation.4 | async-start | bytes 262144 | tf_op jit(solution)/shard_map/all_to_all | solution.py:683
  84.0 3.6 %shard_map.149 = (f32[2,16,16384]{2,1,0:T(8,128)}, f32[2,8,128]{2,1,0:T(8,128)S(1)}, f32[6,8,128]{2,1,0:T(8,128)S(1)}) custom-call(f32[2,16,16384]{2,1,0:T(8,128)} %get-tuple-element.131.refs_0_, s32[1,8,8]{2,1,0:T(8,128)} %refs_1_.11, f32[128,256]{1,0:T(8,128)} %get-tuple-element.144.refs_2_, f32[2,2,64,256]{3,2,1,0:T(8,128)} %get-tuple-element.145.refs_3_, ...), custom_call_target="tpu_custom_call" | custom-call | flops 60000002048 | bytes 180000000 | tf_op jit(solution)/shard_map/pallas_call | solution.py:150
  87.6 4.1 %all-to-all-done.4.refs_0_ = f32[32,8,128]{2,1,0:T(8,128)S(1)} async-done(((f32[32,8,128]{2,1,0:T(8,128)}), f32[32,8,128]{2,1,0:T(8,128)S(1)}, u32[]{:S(2)}, u32[]{:S(2)}) %all-to-all-start.4) | async-done | bytes 131104 | tf_op jit(solution)/shard_map/all_to_all | solution.py:683
  91.7 1.0 %shard_map.150 = (f32[2,40]{1,0:T(2,128)}, f32[1,40]{1,0:T(1,128)}) custom-call(f32[32,8,128]{2,1,0:T(8,128)S(1)} %all-to-all-done.4.refs_0_, f32[2,8,128]{2,1,0:T(8,128)S(1)} %get-tuple-element.149.refs_1_, f32[6,8,128]{2,1,0:T(8,128)S(1)} %get-tuple-element.150.refs_2_), custom_call_target="tpu_custom_call" | custom-call | flops 60000002048 | bytes 180000000 | tf_op jit(solution)/shard_map/pallas_call | solution.py:150
Async XLA Ops:
  2.8 21.4 %collective-permute-start = (f32[4,64,256]{2,1,0:T(8,128)}, f32[4,64,256]{2,1,0:T(8,128)S(1)}, u32[]{:S(2)}, u32[]{:S(2)}) collective-permute-start(f32[4,64,256]{2,1,0:T(8,128)} %get-tuple-element.82.refs_7_), channel_id=1, source_target_pairs={{0,4},{4,0},{8,12},{12,8},{16,20},{20,16},{24,28},{28,24},{1,5},{5... | collective-permute-start | bytes 786440 | tf_op jit(solution)/shard_map/ppermute | solution.py:686
  5.8 18.4 %collective-permute-start.1 = (f32[4,64,256]{2,1,0:T(8,128)}, f32[4,64,256]{2,1,0:T(8,128)S(1)}, u32[]{:S(2)}, u32[]{:S(2)}) collective-permute-start(f32[4,64,256]{2,1,0:T(8,128)} %get-tuple-element.83.refs_8_), channel_id=1, source_target_pairs={{4,8},{8,4},{12,16},{16,12},{20,24},{24,20},{5,9},{9,5},{13,17},{1... | collective-permute-start | bytes 786440 | tf_op jit(solution)/shard_map/ppermute | solution.py:686
  9.9 14.3 %all-to-all-start = ((f32[8,8,128]{2,1,0:T(8,128)}), f32[8,8,128]{2,1,0:T(8,128)S(1)}, u32[]{:S(2)}, u32[]{:S(2)}) async-start(f32[8,8,128]{2,1,0:T(8,128)} %get-tuple-element.85), calls=%async_computation | async-start | bytes 65536 | tf_op jit(solution)/shard_map/all_to_all | solution.py:683
  25.8 13.6 %all-to-all-start.1 = ((f32[8,8,128]{2,1,0:T(8,128)}), f32[8,8,128]{2,1,0:T(8,128)S(1)}, u32[]{:S(2)}, u32[]{:S(2)}) async-start(f32[8,8,128]{2,1,0:T(8,128)} %get-tuple-element.100), calls=%async_computation.1 | async-start | bytes 65536 | tf_op jit(solution)/shard_map/all_to_all | solution.py:683
  30.6 8.8 %collective-permute-start.2 = (f32[2,64,256]{2,1,0:T(8,128)}, f32[2,64,256]{2,1,0:T(8,128)S(1)}, u32[]{:S(2)}, u32[]{:S(2)}) collective-permute-start(f32[2,64,256]{2,1,0:T(8,128)} %get-tuple-element.101), channel_id=1, source_target_pairs={{0,4},{4,0},{8,12},{12,8},{16,20},{20,16},{24,28},{28,24},{1,5},{5... | collective-permute-start | bytes 393224 | tf_op jit(solution)/shard_map/ppermute | solution.py:686
  32.6 6.8 %collective-permute-start.3 = (f32[2,64,256]{2,1,0:T(8,128)}, f32[2,64,256]{2,1,0:T(8,128)S(1)}, u32[]{:S(2)}, u32[]{:S(2)}) collective-permute-start(f32[2,64,256]{2,1,0:T(8,128)} %get-tuple-element.102), channel_id=1, source_target_pairs={{4,8},{8,4},{12,16},{16,12},{20,24},{24,20},{5,9},{9,5},{13,17},{1... | collective-permute-start | bytes 393224 | tf_op jit(solution)/shard_map/ppermute | solution.py:686
  41.1 16.2 %all-to-all-start.2 = ((f32[8,8,128]{2,1,0:T(8,128)}), f32[8,8,128]{2,1,0:T(8,128)S(1)}, u32[]{:S(2)}, u32[]{:S(2)}) async-start(f32[8,8,128]{2,1,0:T(8,128)} %get-tuple-element.116), calls=%async_computation.2 | async-start | bytes 65536 | tf_op jit(solution)/shard_map/all_to_all | solution.py:683
  48.3 8.9 %collective-permute-start.4 = (f32[2,64,256]{2,1,0:T(8,128)}, f32[2,64,256]{2,1,0:T(8,128)S(1)}, u32[]{:S(2)}, u32[]{:S(2)}) collective-permute-start(f32[2,64,256]{2,1,0:T(8,128)} %get-tuple-element.117), channel_id=1, source_target_pairs={{0,4},{4,0},{8,12},{12,8},{16,20},{20,16},{24,28},{28,24},{1,5},{5... | collective-permute-start | bytes 393224 | tf_op jit(solution)/shard_map/ppermute | solution.py:686
  50.3 6.9 %collective-permute-start.5 = (f32[2,64,256]{2,1,0:T(8,128)}, f32[2,64,256]{2,1,0:T(8,128)S(1)}, u32[]{:S(2)}, u32[]{:S(2)}) collective-permute-start(f32[2,64,256]{2,1,0:T(8,128)} %get-tuple-element.118), channel_id=1, source_target_pairs={{4,8},{8,4},{12,16},{16,12},{20,24},{24,20},{5,9},{9,5},{13,17},{1... | collective-permute-start | bytes 393224 | tf_op jit(solution)/shard_map/ppermute | solution.py:686
  59.0 16.0 %all-to-all-start.3 = ((f32[8,8,128]{2,1,0:T(8,128)}), f32[8,8,128]{2,1,0:T(8,128)S(1)}, u32[]{:S(2)}, u32[]{:S(2)}) async-start(f32[8,8,128]{2,1,0:T(8,128)} %get-tuple-element.132), calls=%async_computation.3 | async-start | bytes 65536 | tf_op jit(solution)/shard_map/all_to_all | solution.py:683
  66.2 8.8 %collective-permute-start.6 = (f32[2,64,256]{2,1,0:T(8,128)}, f32[2,64,256]{2,1,0:T(8,128)S(1)}, u32[]{:S(2)}, u32[]{:S(2)}) collective-permute-start(f32[2,64,256]{2,1,0:T(8,128)} %get-tuple-element.133), channel_id=1, source_target_pairs={{0,4},{4,0},{8,12},{12,8},{16,20},{20,16},{24,28},{28,24},{1,5},{5... | collective-permute-start | bytes 393224 | tf_op jit(solution)/shard_map/ppermute | solution.py:686
  68.2 6.8 %collective-permute-start.7 = (f32[2,64,256]{2,1,0:T(8,128)}, f32[2,64,256]{2,1,0:T(8,128)S(1)}, u32[]{:S(2)}, u32[]{:S(2)}) collective-permute-start(f32[2,64,256]{2,1,0:T(8,128)} %get-tuple-element.134), channel_id=1, source_target_pairs={{4,8},{8,4},{12,16},{16,12},{20,24},{24,20},{5,9},{9,5},{13,17},{1... | collective-permute-start | bytes 393224 | tf_op jit(solution)/shard_map/ppermute | solution.py:686
  76.7 15.0 %all-to-all-start.4 = ((f32[32,8,128]{2,1,0:T(8,128)}), f32[32,8,128]{2,1,0:T(8,128)S(1)}, u32[]{:S(2)}, u32[]{:S(2)}) async-start(f32[32,8,128]{2,1,0:T(8,128)} %get-tuple-element.148), calls=%async_computation.4 | async-start | bytes 262144 | tf_op jit(solution)/shard_map/all_to_all | solution.py:683

commit v2 on v1

--- a/solution.py
+++ b/solution.py
@@ -167,10 +167,8 @@
 
 def side_of(n):
     tile = lax.axis_index("tiles")
-    odd = tile % 2
-    side = 1 - odd if n == 0 else odd
-    there = jnp.where(side == 0, tile > 0, tile < lax.axis_size("tiles") - 1)
-    return side, jnp.where(there, 1.0, 0.0)
+    there = tile > 0 if n == 0 else tile < lax.axis_size("tiles") - 1
+    return n, jnp.where(there, 1.0, 0.0)
 
 
 def pack_kernel(z, k):
@@ -324,6 +322,8 @@
     for n in range(1, z.NT):
         payload[n] = payload[0]
     k.o.payload.send()
+    one_hots(z, k)
+    send(k.o.near, k.o.near_edges)
     table = k.i.table.v[...]
     for p in range(parts):
         coming[p].wait()
@@ -335,8 +335,6 @@
 
         lax.fori_loop(0, size // LANES, look, 0, unroll=16)
         k.stores.append(k.copy(inv.at[:, columns[p]], k.o.inv.h.at[:, columns[p]]))
-    one_hots(z, k)
-    send(k.o.near, k.o.near_edges)
 
 
 def one_hots(z, k):
@@ -676,14 +674,14 @@
     wide_tile = pltpu.VMEM((z.M, z.R, z.W + 2 * LANES), F32)
     wide_rows = pltpu.VMEM((z.R, z.W + 2 * LANES), F32)
     plain_tile = pltpu.VMEM(tile_shape, F32)
-    partner = [i ^ 1 for i in range(z.NT)], [((i + 1) ^ 1) - 1 for i in range(z.NT)]
-    pairs = [[(i, j) for i, j in enumerate(js) if 0 <= j < z.NT] for js in partner]
+    onward = [(i, (i + 1) % z.NT) for i in range(z.NT)]
+    back = [(j, i) for i, j in onward]
 
     def share(x, axes):
         return lax.all_to_all(x, axes, 0, 0, tiled=True)
 
-    def swap(x, y):
-        return lax.ppermute(x, "tiles", pairs[0]), lax.ppermute(y, "tiles", pairs[1])
+    def swap(top, bottom):
+        return lax.ppermute(bottom, "tiles", onward), lax.ppermute(top, "tiles", back)
 
     edges_shape = (2,) + edge_shape
     level_buffer = pltpu.VMEM((z.SR, LANES), F32)

time: 93.5 us -> 87.9 us (0.940)
  starting transfers between devices: 46 us -> 41.1 us
    all_to_all x5, starting transfers between devices: 34.2 us -> 20.8 us  [share(): return lax.all_to_all(x, axes, 0, 0, tiled=True)]
    ppermute x8, starting transfers between devices: 11.9 us -> 20.3 us  [the longest x4 14.4 us: swap(): lax.ppermute(top, 'tiles', back)]
  transfers between devices with their start and end apart: 13 -> 13, of which waited for: 2 -> 2; matrix products, arithmetic and copies ran while one was open for 0% -> 0% of each run, Pallas kernels for 33% -> 35%
where the time goes in v2:
time: 87.9 us; the launch traced here: 87.3 us
  starting transfers between devices  41.1 us (47%)
  Pallas kernels  39.9 us (45%)
  waiting for transfers between devices  5.33 us (6%)
  between operations  0.98 us (1%)
    pallas_call x12, Pallas kernels, staged_call(): pl.pallas_call(kernel, out_shape=[(pltpu.VMEM if here else pltpu.HBM)(x.x...  39.9 us
    all_to_all x5, starting transfers between devices, share(): return lax.all_to_all(x, axes, 0, 0, tiled=True)  20.8 us
    ppermute x4, starting transfers between devices, swap(): lax.ppermute(top, 'tiles', back)  14.4 us
    ppermute x4, starting transfers between devices, swap(): lax.ppermute(bottom, 'tiles', onward)  5.91 us
    all_to_all x5, waiting for transfers between devices, share(): return lax.all_to_all(x, axes, 0, 0, tiled=True)  5.3 us
  transfers between devices with their start and end apart: 13, of which 2 were waited for; matrix products, arithmetic and copies ran while one was open for 0% of the time, Pallas kernels for 35%

profile of v2, /device:TPU:0, one launch (start us, length us, event | category | flops | bytes accessed | tf_op | source)
XLA Modules:
  0.0 87.3 jit_solution(17904796749800290391)
XLA Ops:
  0.6 2.2 %shard_map.139 = (f32[4,64,256]{2,1,0:T(8,128)}, f32[4,64,256]{2,1,0:T(8,128)}, f32[16,128]{1,0:T(8,128)}) custom-call(f32[2,16,16384]{2,1,0:T(8,128)} %refs_0_.5, f32[16,16384]{1,0:T(8,128)} %refs_4_.9, s32[16,16384]{1,0:T(8,128)} %refs_0_.4, f32[16]{0:T(128)} %refs_3_.2), custom_call_target="tpu_custom_call" | custom-call | flops 60000002048 | bytes 180000000 | tf_op jit(solution)/shard_map/pallas_call | solution.py:150
  2.8 6.0 %collective-permute-start.1 = (f32[4,64,256]{2,1,0:T(8,128)}, f32[4,64,256]{2,1,0:T(8,128)S(1)}, u32[]{:S(2)}, u32[]{:S(2)}) collective-permute-start(f32[4,64,256]{2,1,0:T(8,128)} %get-tuple-element.82.refs_7_), channel_id=1, source_target_pairs={{4,0},{8,4},{12,8},{16,12},{20,16},{24,20},{28,24},{0,28},{5,1},{9... | collective-permute-start | bytes 786440 | tf_op jit(solution)/shard_map/ppermute | solution.py:684
  8.8 0.0 collective-permute-start
  8.8 3.2 %shard_map.140 = (f32[8,8,128]{2,1,0:T(8,128)}, f32[16,16384]{1,0:T(8,128)}, f32[3,64,128]{2,1,0:T(8,128)}, f32[6,64,128]{2,1,0:T(8,128)}) custom-call(s32[16,16384]{1,0:T(8,128)} %refs_0_.4, f32[16,128]{1,0:T(8,128)} %get-tuple-element.78.refs_1_, s32[1,8,8]{2,1,0:T(8,128)} %refs_1_.11, s32[1,8,8]{2,1,0:T(8,128)} %refs_3_.3, s32[320]{0:T(512)} %refs_4_.5, ...), custom_call_target="tpu_custom_call" | custom-call | flops 60000002048 | bytes 180000000 | tf_op jit(solution)/shard_map/pallas_call | solution.py:150
  12.0 6.0 %all-to-all-start = ((f32[8,8,128]{2,1,0:T(8,128)}), f32[8,8,128]{2,1,0:T(8,128)S(1)}, u32[]{:S(2)}, u32[]{:S(2)}) async-start(f32[8,8,128]{2,1,0:T(8,128)} %get-tuple-element.85), calls=%async_computation | async-start | bytes 65536 | tf_op jit(solution)/shard_map/all_to_all | solution.py:681
  18.0 5.5 %shard_map.141 = (f32[64,256]{1,0:T(8,128)S(1)}, f32[64,256]{1,0:T(8,128)}, f32[2,16,16384]{2,1,0:T(8,128)}, f32[128,256]{1,0:T(8,128)S(1)}, f32[2,2,64,256]{3,2...) custom-call(f32[2,16,16384]{2,1,0:T(8,128)} %refs_0_.5, ...), custom_call_target="tpu_custom_call" | custom-call | flops 60000002048 | bytes 180000000 | tf_op jit(solution)/shard_map/pallas_call | solution.py:150
  23.5 1.2 %all-to-all-done.refs_0_ = f32[8,8,128]{2,1,0:T(8,128)S(1)} async-done(((f32[8,8,128]{2,1,0:T(8,128)}), f32[8,8,128]{2,1,0:T(8,128)S(1)}, u32[]{:S(2)}, u32[]{:S(2)}) %all-to-all-start) | async-done | bytes 32800 | tf_op jit(solution)/shard_map/all_to_all | solution.py:681
  24.7 0.0 collective-permute-done.1.refs_2_
  24.7 0.0 collective-permute-done.refs_1_
  24.7 1.5 %shard_map.142 = (f32[8,8,128]{2,1,0:T(8,128)}, f32[2,4,64,256]{3,2,1,0:T(8,128)}, f32[6,8,128]{2,1,0:T(8,128)}, f32[2,2,64,256]{3,2,1,0:T(8,128)}, f32[128,256]...) custom-call(f32[8,8,128]{2,1,0:T(8,128)S(1)} %all-to-all-done.refs_0_, ...), custom_call_target="tpu_custom_call" | custom-call | flops 60000002048 | bytes 180000000 | tf_op jit(solution)/shard_map/pallas_call | solution.py:150
  26.2 4.8 %all-to-all-start.1 = ((f32[8,8,128]{2,1,0:T(8,128)}), f32[8,8,128]{2,1,0:T(8,128)S(1)}, u32[]{:S(2)}, u32[]{:S(2)}) async-start(f32[8,8,128]{2,1,0:T(8,128)} %get-tuple-element.100), calls=%async_computation.1 | async-start | bytes 65536 | tf_op jit(solution)/shard_map/all_to_all | solution.py:681
  31.0 2.0 %collective-permute-start.2 = (f32[2,64,256]{2,1,0:T(8,128)}, f32[2,64,256]{2,1,0:T(8,128)S(1)}, u32[]{:S(2)}, u32[]{:S(2)}) collective-permute-start(f32[2,64,256]{2,1,0:T(8,128)} %get-tuple-element.101), channel_id=1, source_target_pairs={{0,4},{4,8},{8,12},{12,16},{16,20},{20,24},{24,28},{28,0},{1,5},{5... | collective-permute-start | bytes 393224 | tf_op jit(solution)/shard_map/ppermute | solution.py:684
  33.1 2.7 %collective-permute-start.3 = (f32[2,64,256]{2,1,0:T(8,128)}, f32[2,64,256]{2,1,0:T(8,128)S(1)}, u32[]{:S(2)}, u32[]{:S(2)}) collective-permute-start(f32[2,64,256]{2,1,0:T(8,128)} %get-tuple-element.102), channel_id=1, source_target_pairs={{4,0},{8,4},{12,8},{16,12},{20,16},{24,20},{28,24},{0,28},{5,1},{9... | collective-permute-start | bytes 393224 | tf_op jit(solution)/shard_map/ppermute | solution.py:684
  35.8 6.1 %shard_map.143 = (f32[2,16,16384]{2,1,0:T(8,128)}, f32[128,256]{1,0:T(8,128)S(1)}, f32[2,2,64,256]{3,2,1,0:T(8,128)S(1)}, f32[2,8,128]{2,1,0:T(8,128)S(1)}, f32[...) custom-call(f32[2,16,16384]{2,1,0:T(8,128)} %get-tuple-element.84.re, ...), custom_call_target="tpu_custom_call" | custom-call | flops 60000002048 | bytes 180000000 | tf_op jit(solution)/shard_map/pallas_call | solution.py:150
  41.9 0.0 all-to-all-done.1.refs_0_
  41.9 0.0 collective-permute-done.2.refs_1_
  41.9 0.0 collective-permute-done.3.refs_2_
  41.9 1.6 %shard_map.144 = (f32[8,8,128]{2,1,0:T(8,128)}, f32[2,2,64,256]{3,2,1,0:T(8,128)}, f32[128,256]{1,0:T(8,128)}, f32[2,8,128]{2,1,0:T(8,128)}, f32[2,64,256]{2,1,0:T(8,128)}, /*index=5*/f32[2,64,256]{2,1,0:T(8,128)}) custom-call(f32[8,8,128]{2,1,0:T(8,128)S(1)} %all-to-all-done.1.refs_0_, f32[2,64,256]{2,1,0:T(8,128)S(1)} %collective-permute-done.2.refs_1_, ...), custom_call_target="tpu_custom_call" | custom-call | flops 60000002048 | bytes 180000000 | tf_op jit(solution)/shard_map/pallas_call | solution.py:150
  43.5 3.3 %all-to-all-start.2 = ((f32[8,8,128]{2,1,0:T(8,128)}), f32[8,8,128]{2,1,0:T(8,128)S(1)}, u32[]{:S(2)}, u32[]{:S(2)}) async-start(f32[8,8,128]{2,1,0:T(8,128)} %get-tuple-element.116), calls=%async_computation.2 | async-start | bytes 65536 | tf_op jit(solution)/shard_map/all_to_all | solution.py:681
  46.9 2.0 %collective-permute-start.4 = (f32[2,64,256]{2,1,0:T(8,128)}, f32[2,64,256]{2,1,0:T(8,128)S(1)}, u32[]{:S(2)}, u32[]{:S(2)}) collective-permute-start(f32[2,64,256]{2,1,0:T(8,128)} %get-tuple-element.117), channel_id=1, source_target_pairs={{0,4},{4,8},{8,12},{12,16},{16,20},{20,24},{24,28},{28,0},{1,5},{5... | collective-permute-start | bytes 393224 | tf_op jit(solution)/shard_map/ppermute | solution.py:684
  48.8 2.8 %collective-permute-start.5 = (f32[2,64,256]{2,1,0:T(8,128)}, f32[2,64,256]{2,1,0:T(8,128)S(1)}, u32[]{:S(2)}, u32[]{:S(2)}) collective-permute-start(f32[2,64,256]{2,1,0:T(8,128)} %get-tuple-element.118), channel_id=1, source_target_pairs={{4,0},{8,4},{12,8},{16,12},{20,16},{24,20},{28,24},{0,28},{5,1},{9... | collective-permute-start | bytes 393224 | tf_op jit(solution)/shard_map/ppermute | solution.py:684
  51.6 6.0 %shard_map.145 = (f32[2,16,16384]{2,1,0:T(8,128)}, f32[128,256]{1,0:T(8,128)S(1)}, f32[2,2,64,256]{3,2,1,0:T(8,128)S(1)}, f32[2,8,128]{2,1,0:T(8,128)S(1)}, f32[...) custom-call(f32[2,16,16384]{2,1,0:T(8,128)} %get-tuple-element.99.re, ...), custom_call_target="tpu_custom_call" | custom-call | flops 60000002048 | bytes 180000000 | tf_op jit(solution)/shard_map/pallas_call | solution.py:150
  57.7 0.0 all-to-all-done.2.refs_0_
  57.7 0.0 collective-permute-done.4.refs_1_
  57.7 0.0 collective-permute-done.5.refs_2_
  57.7 1.6 %shard_map.146 = (f32[8,8,128]{2,1,0:T(8,128)}, f32[2,2,64,256]{3,2,1,0:T(8,128)}, f32[128,256]{1,0:T(8,128)}, f32[2,8,128]{2,1,0:T(8,128)}, f32[2,64,256]{2,1,0:T(8,128)}, /*index=5*/f32[2,64,256]{2,1,0:T(8,128)}) custom-call(f32[8,8,128]{2,1,0:T(8,128)S(1)} %all-to-all-done.2.refs_0_, f32[2,64,256]{2,1,0:T(8,128)S(1)} %collective-permute-done.4.refs_1_, ...), custom_call_target="tpu_custom_call" | custom-call | flops 60000002048 | bytes 180000000 | tf_op jit(solution)/shard_map/pallas_call | solution.py:150
  59.3 3.3 %all-to-all-start.3 = ((f32[8,8,128]{2,1,0:T(8,128)}), f32[8,8,128]{2,1,0:T(8,128)S(1)}, u32[]{:S(2)}, u32[]{:S(2)}) async-start(f32[8,8,128]{2,1,0:T(8,128)} %get-tuple-element.132), calls=%async_computation.3 | async-start | bytes 65536 | tf_op jit(solution)/shard_map/all_to_all | solution.py:681
  62.7 1.9 %collective-permute-start.6 = (f32[2,64,256]{2,1,0:T(8,128)}, f32[2,64,256]{2,1,0:T(8,128)S(1)}, u32[]{:S(2)}, u32[]{:S(2)}) collective-permute-start(f32[2,64,256]{2,1,0:T(8,128)} %get-tuple-element.133), channel_id=1, source_target_pairs={{0,4},{4,8},{8,12},{12,16},{16,20},{20,24},{24,28},{28,0},{1,5},{5... | collective-permute-start | bytes 393224 | tf_op jit(solution)/shard_map/ppermute | solution.py:684
  64.6 2.9 %collective-permute-start.7 = (f32[2,64,256]{2,1,0:T(8,128)}, f32[2,64,256]{2,1,0:T(8,128)S(1)}, u32[]{:S(2)}, u32[]{:S(2)}) collective-permute-start(f32[2,64,256]{2,1,0:T(8,128)} %get-tuple-element.134), channel_id=1, source_target_pairs={{4,0},{8,4},{12,8},{16,12},{20,16},{24,20},{28,24},{0,28},{5,1},{9... | collective-permute-start | bytes 393224 | tf_op jit(solution)/shard_map/ppermute | solution.py:684
  67.5 6.1 %shard_map.147 = (f32[2,16,16384]{2,1,0:T(8,128)}, f32[128,256]{1,0:T(8,128)S(1)}, f32[2,2,64,256]{3,2,1,0:T(8,128)S(1)}, f32[2,8,128]{2,1,0:T(8,128)S(1)}, f32[...) custom-call(f32[2,16,16384]{2,1,0:T(8,128)} %get-tuple-element.115.r, ...), custom_call_target="tpu_custom_call" | custom-call | flops 60000002048 | bytes 180000000 | tf_op jit(solution)/shard_map/pallas_call | solution.py:150
  73.5 0.0 all-to-all-done.3.refs_0_
  73.5 0.0 collective-permute-done.6.refs_1_
  73.6 0.0 collective-permute-done.7.refs_2_
  73.6 1.6 %shard_map.148 = (f32[32,8,128]{2,1,0:T(8,128)}, f32[2,2,64,256]{3,2,1,0:T(8,128)}, f32[128,256]{1,0:T(8,128)}, f32[2,8,128]{2,1,0:T(8,128)}) custom-call(f32[8,8,128]{2,1,0:T(8,128)S(1)} %all-to-all-done.3.refs_0_, f32[2,64,256]{2,1,0:T(8,128)S(1)} %collective-permute-done.6.refs_1_, f32[2,64,256]{2,1,0:T(8,128)S(1)} %collective-permute-done.7.refs_2_, ...), custom_call_target="tpu_custom_call" | custom-call | flops 60000002048 | bytes 180000000 | tf_op jit(solution)/shard_map/pallas_call | solution.py:150
  75.2 3.2 %all-to-all-start.4 = ((f32[32,8,128]{2,1,0:T(8,128)}), f32[32,8,128]{2,1,0:T(8,128)S(1)}, u32[]{:S(2)}, u32[]{:S(2)}) async-start(f32[32,8,128]{2,1,0:T(8,128)} %get-tuple-element.148), calls=%async_computation.4 | async-start | bytes 262144 | tf_op jit(solution)/shard_map/all_to_all | solution.py:681
  78.4 3.6 %shard_map.149 = (f32[2,16,16384]{2,1,0:T(8,128)}, f32[2,8,128]{2,1,0:T(8,128)S(1)}, f32[6,8,128]{2,1,0:T(8,128)S(1)}) custom-call(f32[2,16,16384]{2,1,0:T(8,128)} %get-tuple-element.131.refs_0_, s32[1,8,8]{2,1,0:T(8,128)} %refs_1_.11, f32[128,256]{1,0:T(8,128)} %get-tuple-element.144.refs_2_, f32[2,2,64,256]{3,2,1,0:T(8,128)} %get-tuple-element.145.refs_3_, ...), custom_call_target="tpu_custom_call" | custom-call | flops 60000002048 | bytes 180000000 | tf_op jit(solution)/shard_map/pallas_call | solution.py:150
  82.1 4.1 %all-to-all-done.4.refs_0_ = f32[32,8,128]{2,1,0:T(8,128)S(1)} async-done(((f32[32,8,128]{2,1,0:T(8,128)}), f32[32,8,128]{2,1,0:T(8,128)S(1)}, u32[]{:S(2)}, u32[]{:S(2)}) %all-to-all-start.4) | async-done | bytes 131104 | tf_op jit(solution)/shard_map/all_to_all | solution.py:681
  86.2 1.0 %shard_map.150 = (f32[2,40]{1,0:T(2,128)}, f32[1,40]{1,0:T(1,128)}) custom-call(f32[32,8,128]{2,1,0:T(8,128)S(1)} %all-to-all-done.4.refs_0_, f32[2,8,128]{2,1,0:T(8,128)S(1)} %get-tuple-element.149.refs_1_, f32[6,8,128]{2,1,0:T(8,128)S(1)} %get-tuple-element.150.refs_2_), custom_call_target="tpu_custom_call" | custom-call | flops 60000002048 | bytes 180000000 | tf_op jit(solution)/shard_map/pallas_call | solution.py:150
Async XLA Ops:
  2.8 21.9 %collective-permute-start.1 = (f32[4,64,256]{2,1,0:T(8,128)}, f32[4,64,256]{2,1,0:T(8,128)S(1)}, u32[]{:S(2)}, u32[]{:S(2)}) collective-permute-start(f32[4,64,256]{2,1,0:T(8,128)} %get-tuple-element.82.refs_7_), channel_id=1, source_target_pairs={{4,0},{8,4},{12,8},{16,12},{20,16},{24,20},{28,24},{0,28},{5,1},{9... | collective-permute-start | bytes 786440 | tf_op jit(solution)/shard_map/ppermute | solution.py:684
  8.8 15.9 %collective-permute-start = (f32[4,64,256]{2,1,0:T(8,128)}, f32[4,64,256]{2,1,0:T(8,128)S(1)}, u32[]{:S(2)}, u32[]{:S(2)}) collective-permute-start(f32[4,64,256]{2,1,0:T(8,128)} %get-tuple-element.83.refs_8_), channel_id=1, source_target_pairs={{0,4},{4,8},{8,12},{12,16},{16,20},{20,24},{24,28},{28,0},{1,5},{5... | collective-permute-start | bytes 786440 | tf_op jit(solution)/shard_map/ppermute | solution.py:684
  12.0 12.7 %all-to-all-start = ((f32[8,8,128]{2,1,0:T(8,128)}), f32[8,8,128]{2,1,0:T(8,128)S(1)}, u32[]{:S(2)}, u32[]{:S(2)}) async-start(f32[8,8,128]{2,1,0:T(8,128)} %get-tuple-element.85), calls=%async_computation | async-start | bytes 65536 | tf_op jit(solution)/shard_map/all_to_all | solution.py:681
  26.2 15.7 %all-to-all-start.1 = ((f32[8,8,128]{2,1,0:T(8,128)}), f32[8,8,128]{2,1,0:T(8,128)S(1)}, u32[]{:S(2)}, u32[]{:S(2)}) async-start(f32[8,8,128]{2,1,0:T(8,128)} %get-tuple-element.100), calls=%async_computation.1 | async-start | bytes 65536 | tf_op jit(solution)/shard_map/all_to_all | solution.py:681
  31.0 10.8 %collective-permute-start.2 = (f32[2,64,256]{2,1,0:T(8,128)}, f32[2,64,256]{2,1,0:T(8,128)S(1)}, u32[]{:S(2)}, u32[]{:S(2)}) collective-permute-start(f32[2,64,256]{2,1,0:T(8,128)} %get-tuple-element.101), channel_id=1, source_target_pairs={{0,4},{4,8},{8,12},{12,16},{16,20},{20,24},{24,28},{28,0},{1,5},{5... | collective-permute-start | bytes 393224 | tf_op jit(solution)/shard_map/ppermute | solution.py:684
  33.1 8.8 %collective-permute-start.3 = (f32[2,64,256]{2,1,0:T(8,128)}, f32[2,64,256]{2,1,0:T(8,128)S(1)}, u32[]{:S(2)}, u32[]{:S(2)}) collective-permute-start(f32[2,64,256]{2,1,0:T(8,128)} %get-tuple-element.102), channel_id=1, source_target_pairs={{4,0},{8,4},{12,8},{16,12},{20,16},{24,20},{28,24},{0,28},{5,1},{9... | collective-permute-start | bytes 393224 | tf_op jit(solution)/shard_map/ppermute | solution.py:684
  43.5 14.2 %all-to-all-start.2 = ((f32[8,8,128]{2,1,0:T(8,128)}), f32[8,8,128]{2,1,0:T(8,128)S(1)}, u32[]{:S(2)}, u32[]{:S(2)}) async-start(f32[8,8,128]{2,1,0:T(8,128)} %get-tuple-element.116), calls=%async_computation.2 | async-start | bytes 65536 | tf_op jit(solution)/shard_map/all_to_all | solution.py:681
  46.9 10.8 %collective-permute-start.4 = (f32[2,64,256]{2,1,0:T(8,128)}, f32[2,64,256]{2,1,0:T(8,128)S(1)}, u32[]{:S(2)}, u32[]{:S(2)}) collective-permute-start(f32[2,64,256]{2,1,0:T(8,128)} %get-tuple-element.117), channel_id=1, source_target_pairs={{0,4},{4,8},{8,12},{12,16},{16,20},{20,24},{24,28},{28,0},{1,5},{5... | collective-permute-start | bytes 393224 | tf_op jit(solution)/shard_map/ppermute | solution.py:684
  48.8 8.9 %collective-permute-start.5 = (f32[2,64,256]{2,1,0:T(8,128)}, f32[2,64,256]{2,1,0:T(8,128)S(1)}, u32[]{:S(2)}, u32[]{:S(2)}) collective-permute-start(f32[2,64,256]{2,1,0:T(8,128)} %get-tuple-element.118), channel_id=1, source_target_pairs={{4,0},{8,4},{12,8},{16,12},{20,16},{24,20},{28,24},{0,28},{5,1},{9... | collective-permute-start | bytes 393224 | tf_op jit(solution)/shard_map/ppermute | solution.py:684
  59.3 14.2 %all-to-all-start.3 = ((f32[8,8,128]{2,1,0:T(8,128)}), f32[8,8,128]{2,1,0:T(8,128)S(1)}, u32[]{:S(2)}, u32[]{:S(2)}) async-start(f32[8,8,128]{2,1,0:T(8,128)} %get-tuple-element.132), calls=%async_computation.3 | async-start | bytes 65536 | tf_op jit(solution)/shard_map/all_to_all | solution.py:681
  62.7 10.9 %collective-permute-start.6 = (f32[2,64,256]{2,1,0:T(8,128)}, f32[2,64,256]{2,1,0:T(8,128)S(1)}, u32[]{:S(2)}, u32[]{:S(2)}) collective-permute-start(f32[2,64,256]{2,1,0:T(8,128)} %get-tuple-element.133), channel_id=1, source_target_pairs={{0,4},{4,8},{8,12},{12,16},{16,20},{20,24},{24,28},{28,0},{1,5},{5... | collective-permute-start | bytes 393224 | tf_op jit(solution)/shard_map/ppermute | solution.py:684
  64.6 9.0 %collective-permute-start.7 = (f32[2,64,256]{2,1,0:T(8,128)}, f32[2,64,256]{2,1,0:T(8,128)S(1)}, u32[]{:S(2)}, u32[]{:S(2)}) collective-permute-start(f32[2,64,256]{2,1,0:T(8,128)} %get-tuple-element.134), channel_id=1, source_target_pairs={{4,0},{8,4},{12,8},{16,12},{20,16},{24,20},{28,24},{0,28},{5,1},{9... | collective-permute-start | bytes 393224 | tf_op jit(solution)/shard_map/ppermute | solution.py:684
  75.2 11.0 %all-to-all-start.4 = ((f32[32,8,128]{2,1,0:T(8,128)}), f32[32,8,128]{2,1,0:T(8,128)S(1)}, u32[]{:S(2)}, u32[]{:S(2)}) async-start(f32[32,8,128]{2,1,0:T(8,128)} %get-tuple-element.148), calls=%async_computation.4 | async-start | bytes 262144 | tf_op jit(solution)/shard_map/all_to_all | solution.py:681

commit v3 on v2

--- a/solution.py
+++ b/solution.py
@@ -688,7 +688,7 @@
     opened = staged_call(
         pack_kernel, z,
         dict(depth=Raw(depth), bed=Raw(bed), cls=Raw(rough_class), class_n=Scalars(class_n)),
-        dict(pack0=pack_shape, pack1=pack_shape, table=(z.R, LANES)),
+        dict(pack1=pack_shape, pack0=pack_shape, table=(z.R, LANES)),
         dict(rows=pltpu.VMEM((2, z.M + 1, z.W), F32), cls_rows=pltpu.VMEM((2, 1, z.W), I32), ids=pltpu.VMEM((z.PR, SEG), I32)),
         extra_sems=2 * (z.M + 2),
     )
@@ -709,7 +709,7 @@
     flow = staged_call(
         functools.partial(flow_kernel, first=True), z,
         dict(wet=Raw(depth), seg=Scalars(contact_seg), bed=Raw(bed), inv=Raw(inv), rain=Raw(rain), near=Passed(near),
-             near_edges=Passed(near_edges), own0=Passed(opened.pack0), own1=Passed(opened.pack1)),
+             near_edges=Passed(near_edges), own1=Passed(opened.pack1), own0=Passed(opened.pack0)),
         dict(bed_c=Here((z.C, SEG)), bed_kept=Raw((z.C, SEG)), **flow_out),
         dict(bed_c=pltpu.VMEM((z.C, SEG), F32), **flow_scratch),
         extra_sems=5 * blocks + 1,
@@ -720,8 +720,8 @@
     exchange_out = dict(edge0=Raw(edge_shape), edge1=Raw(edge_shape))
     now = staged_call(
         open_kernel, z,
-        dict(got=Here(got, free=True), from0=Here(from0, free=True), from1=Here(from1, free=True), own0=Here(flow.own0),
-             own1=Here(flow.own1), edges=Here(flow.edges), near=Here(flow.near), near_edges=Here(flow.near_edges),
+        dict(got=Here(got, free=True), from1=Here(from1, free=True), from0=Here(from0, free=True), own1=Here(flow.own1),
+             own0=Here(flow.own0), edges=Here(flow.edges), near=Here(flow.near), near_edges=Here(flow.near_edges),
              wet_c=Here(flow.wet_c), bed_c=Here(flow.bed_c)),
         dict(payload=(z.NT, z.SR, LANES), pack=(2, 4, z.PR, SEG), consts=const_shape, **step_out, **exchange_out),
         dict(pool=level_buffer, level=level_buffer),

time: 87.9 us -> 85.4 us (0.972)
  starting transfers between devices: 41.1 us -> 38.6 us
    ppermute x4, starting transfers between devices: 5.91 us -> 8.89 us  [swap(): lax.ppermute(bottom, 'tiles', onward)]
    ppermute x4, starting transfers between devices: 14.4 us -> 11.5 us  [swap(): lax.ppermute(top, 'tiles', back)]
    all_to_all x5, starting transfers between devices: 20.8 us -> 18.2 us  [share(): return lax.all_to_all(x, axes, 0, 0, tiled=True)]
  transfers between devices with their start and end apart: 13 -> 13, of which waited for: 2 -> 2; matrix products, arithmetic and copies ran while one was open for 0% -> 0% of each run, Pallas kernels for 35% -> 36%
where the time goes in v3:
time: 85.4 us; the launch traced here: 84.7 us
  Pallas kernels  39.9 us (47%)
  starting transfers between devices  38.6 us (45%)
  waiting for transfers between devices  5.25 us (6%)
  between operations  0.99 us (1%)
    pallas_call x12, Pallas kernels, staged_call(): pl.pallas_call(kernel, out_shape=[(pltpu.VMEM if here else pltpu.HBM)(x.x...  39.9 us
    all_to_all x5, starting transfers between devices, share(): return lax.all_to_all(x, axes, 0, 0, tiled=True)  18.2 us
    ppermute x4, starting transfers between devices, swap(): lax.ppermute(top, 'tiles', back)  11.5 us
    ppermute x4, starting transfers between devices, swap(): lax.ppermute(bottom, 'tiles', onward)  8.89 us
    all_to_all x5, waiting for transfers between devices, share(): return lax.all_to_all(x, axes, 0, 0, tiled=True)  5.22 us
  transfers between devices with their start and end apart: 13, of which 2 were waited for; matrix products, arithmetic and copies ran while one was open for 0% of the time, Pallas kernels for 36%

profile of v3, /device:TPU:0, one launch (start us, length us, event | category | flops | bytes accessed | tf_op | source)
XLA Modules:
  0.0 84.7 jit_solution(6739633973978619170)
XLA Ops:
  0.6 2.1 %shard_map.139 = (f32[4,64,256]{2,1,0:T(8,128)}, f32[4,64,256]{2,1,0:T(8,128)}, f32[16,128]{1,0:T(8,128)}) custom-call(f32[2,16,16384]{2,1,0:T(8,128)} %refs_0_.5, f32[16,16384]{1,0:T(8,128)} %refs_4_.9, s32[16,16384]{1,0:T(8,128)} %refs_0_.4, f32[16]{0:T(128)} %refs_3_.2), custom_call_target="tpu_custom_call" | custom-call | flops 60000002048 | bytes 180000000 | tf_op jit(solution)/shard_map/pallas_call | solution.py:150
  2.8 3.0 %collective-permute-start.1 = (f32[4,64,256]{2,1,0:T(8,128)}, f32[4,64,256]{2,1,0:T(8,128)S(1)}, u32[]{:S(2)}, u32[]{:S(2)}) collective-permute-start(f32[4,64,256]{2,1,0:T(8,128)} %get-tuple-element.82.refs_7_), channel_id=1, source_target_pairs={{0,4},{4,8},{8,12},{12,16},{16,20},{20,24},{24,28},{28,0},{1,5},{5... | collective-permute-start | bytes 786440 | tf_op jit(solution)/shard_map/ppermute | solution.py:684
  5.8 3.1 %collective-permute-start = (f32[4,64,256]{2,1,0:T(8,128)}, f32[4,64,256]{2,1,0:T(8,128)S(1)}, u32[]{:S(2)}, u32[]{:S(2)}) collective-permute-start(f32[4,64,256]{2,1,0:T(8,128)} %get-tuple-element.83.refs_8_), channel_id=1, source_target_pairs={{4,0},{8,4},{12,8},{16,12},{20,16},{24,20},{28,24},{0,28},{5,1},{9... | collective-permute-start | bytes 786440 | tf_op jit(solution)/shard_map/ppermute | solution.py:684
  8.9 3.2 %shard_map.140 = (f32[8,8,128]{2,1,0:T(8,128)}, f32[16,16384]{1,0:T(8,128)}, f32[3,64,128]{2,1,0:T(8,128)}, f32[6,64,128]{2,1,0:T(8,128)}) custom-call(s32[16,16384]{1,0:T(8,128)} %refs_0_.4, f32[16,128]{1,0:T(8,128)} %get-tuple-element.78.refs_1_, s32[1,8,8]{2,1,0:T(8,128)} %refs_1_.11, s32[1,8,8]{2,1,0:T(8,128)} %refs_3_.3, s32[320]{0:T(512)} %refs_4_.5, ...), custom_call_target="tpu_custom_call" | custom-call | flops 60000002048 | bytes 180000000 | tf_op jit(solution)/shard_map/pallas_call | solution.py:150
  12.1 3.3 %all-to-all-start = ((f32[8,8,128]{2,1,0:T(8,128)}), f32[8,8,128]{2,1,0:T(8,128)S(1)}, u32[]{:S(2)}, u32[]{:S(2)}) async-start(f32[8,8,128]{2,1,0:T(8,128)} %get-tuple-element.85), calls=%async_computation | async-start | bytes 65536 | tf_op jit(solution)/shard_map/all_to_all | solution.py:681
  15.4 5.5 %shard_map.141 = (f32[64,256]{1,0:T(8,128)S(1)}, f32[64,256]{1,0:T(8,128)}, f32[2,16,16384]{2,1,0:T(8,128)}, f32[128,256]{1,0:T(8,128)S(1)}, f32[2,2,64,256]{3,2...) custom-call(f32[2,16,16384]{2,1,0:T(8,128)} %refs_0_.5, ...), custom_call_target="tpu_custom_call" | custom-call | flops 60000002048 | bytes 180000000 | tf_op jit(solution)/shard_map/pallas_call | solution.py:150
  20.9 1.1 %all-to-all-done.refs_0_ = f32[8,8,128]{2,1,0:T(8,128)S(1)} async-done(((f32[8,8,128]{2,1,0:T(8,128)}), f32[8,8,128]{2,1,0:T(8,128)S(1)}, u32[]{:S(2)}, u32[]{:S(2)}) %all-to-all-start) | async-done | bytes 32800 | tf_op jit(solution)/shard_map/all_to_all | solution.py:681
  22.1 0.0 collective-permute-done.1.refs_2_
  22.1 0.0 collective-permute-done.refs_1_
  22.1 1.5 %shard_map.142 = (f32[8,8,128]{2,1,0:T(8,128)}, f32[2,4,64,256]{3,2,1,0:T(8,128)}, f32[6,8,128]{2,1,0:T(8,128)}, f32[2,2,64,256]{3,2,1,0:T(8,128)}, f32[128,256]...) custom-call(f32[8,8,128]{2,1,0:T(8,128)S(1)} %all-to-all-done.refs_0_, ...), custom_call_target="tpu_custom_call" | custom-call | flops 60000002048 | bytes 180000000 | tf_op jit(solution)/shard_map/pallas_call | solution.py:150
  23.6 4.8 %all-to-all-start.1 = ((f32[8,8,128]{2,1,0:T(8,128)}), f32[8,8,128]{2,1,0:T(8,128)S(1)}, u32[]{:S(2)}, u32[]{:S(2)}) async-start(f32[8,8,128]{2,1,0:T(8,128)} %get-tuple-element.100), calls=%async_computation.1 | async-start | bytes 65536 | tf_op jit(solution)/shard_map/all_to_all | solution.py:681
  28.4 2.0 %collective-permute-start.2 = (f32[2,64,256]{2,1,0:T(8,128)}, f32[2,64,256]{2,1,0:T(8,128)S(1)}, u32[]{:S(2)}, u32[]{:S(2)}) collective-permute-start(f32[2,64,256]{2,1,0:T(8,128)} %get-tuple-element.101), channel_id=1, source_target_pairs={{0,4},{4,8},{8,12},{12,16},{16,20},{20,24},{24,28},{28,0},{1,5},{5... | collective-permute-start | bytes 393224 | tf_op jit(solution)/shard_map/ppermute | solution.py:684
  30.4 2.7 %collective-permute-start.3 = (f32[2,64,256]{2,1,0:T(8,128)}, f32[2,64,256]{2,1,0:T(8,128)S(1)}, u32[]{:S(2)}, u32[]{:S(2)}) collective-permute-start(f32[2,64,256]{2,1,0:T(8,128)} %get-tuple-element.102), channel_id=1, source_target_pairs={{4,0},{8,4},{12,8},{16,12},{20,16},{24,20},{28,24},{0,28},{5,1},{9... | collective-permute-start | bytes 393224 | tf_op jit(solution)/shard_map/ppermute | solution.py:684
  33.1 6.1 %shard_map.143 = (f32[2,16,16384]{2,1,0:T(8,128)}, f32[128,256]{1,0:T(8,128)S(1)}, f32[2,2,64,256]{3,2,1,0:T(8,128)S(1)}, f32[2,8,128]{2,1,0:T(8,128)S(1)}, f32[...) custom-call(f32[2,16,16384]{2,1,0:T(8,128)} %get-tuple-element.84.re, ...), custom_call_target="tpu_custom_call" | custom-call | flops 60000002048 | bytes 180000000 | tf_op jit(solution)/shard_map/pallas_call | solution.py:150
  39.2 0.0 all-to-all-done.1.refs_0_
  39.2 0.0 collective-permute-done.2.refs_1_
  39.2 0.0 collective-permute-done.3.refs_2_
  39.2 1.6 %shard_map.144 = (f32[8,8,128]{2,1,0:T(8,128)}, f32[2,2,64,256]{3,2,1,0:T(8,128)}, f32[128,256]{1,0:T(8,128)}, f32[2,8,128]{2,1,0:T(8,128)}, f32[2,64,256]{2,1,0:T(8,128)}, /*index=5*/f32[2,64,256]{2,1,0:T(8,128)}) custom-call(f32[8,8,128]{2,1,0:T(8,128)S(1)} %all-to-all-done.1.refs_0_, f32[2,64,256]{2,1,0:T(8,128)S(1)} %collective-permute-done.2.refs_1_, ...), custom_call_target="tpu_custom_call" | custom-call | flops 60000002048 | bytes 180000000 | tf_op jit(solution)/shard_map/pallas_call | solution.py:150
  40.9 3.3 %all-to-all-start.2 = ((f32[8,8,128]{2,1,0:T(8,128)}), f32[8,8,128]{2,1,0:T(8,128)S(1)}, u32[]{:S(2)}, u32[]{:S(2)}) async-start(f32[8,8,128]{2,1,0:T(8,128)} %get-tuple-element.116), calls=%async_computation.2 | async-start | bytes 65536 | tf_op jit(solution)/shard_map/all_to_all | solution.py:681
  44.2 2.0 %collective-permute-start.4 = (f32[2,64,256]{2,1,0:T(8,128)}, f32[2,64,256]{2,1,0:T(8,128)S(1)}, u32[]{:S(2)}, u32[]{:S(2)}) collective-permute-start(f32[2,64,256]{2,1,0:T(8,128)} %get-tuple-element.117), channel_id=1, source_target_pairs={{0,4},{4,8},{8,12},{12,16},{16,20},{20,24},{24,28},{28,0},{1,5},{5... | collective-permute-start | bytes 393224 | tf_op jit(solution)/shard_map/ppermute | solution.py:684
  46.2 2.8 %collective-permute-start.5 = (f32[2,64,256]{2,1,0:T(8,128)}, f32[2,64,256]{2,1,0:T(8,128)S(1)}, u32[]{:S(2)}, u32[]{:S(2)}) collective-permute-start(f32[2,64,256]{2,1,0:T(8,128)} %get-tuple-element.118), channel_id=1, source_target_pairs={{4,0},{8,4},{12,8},{16,12},{20,16},{24,20},{28,24},{0,28},{5,1},{9... | collective-permute-start | bytes 393224 | tf_op jit(solution)/shard_map/ppermute | solution.py:684
  49.0 6.0 %shard_map.145 = (f32[2,16,16384]{2,1,0:T(8,128)}, f32[128,256]{1,0:T(8,128)S(1)}, f32[2,2,64,256]{3,2,1,0:T(8,128)S(1)}, f32[2,8,128]{2,1,0:T(8,128)S(1)}, f32[...) custom-call(f32[2,16,16384]{2,1,0:T(8,128)} %get-tuple-element.99.re, ...), custom_call_target="tpu_custom_call" | custom-call | flops 60000002048 | bytes 180000000 | tf_op jit(solution)/shard_map/pallas_call | solution.py:150
  55.0 0.0 all-to-all-done.2.refs_0_
  55.0 0.0 collective-permute-done.4.refs_1_
  55.1 0.0 collective-permute-done.5.refs_2_
  55.1 1.6 %shard_map.146 = (f32[8,8,128]{2,1,0:T(8,128)}, f32[2,2,64,256]{3,2,1,0:T(8,128)}, f32[128,256]{1,0:T(8,128)}, f32[2,8,128]{2,1,0:T(8,128)}, f32[2,64,256]{2,1,0:T(8,128)}, /*index=5*/f32[2,64,256]{2,1,0:T(8,128)}) custom-call(f32[8,8,128]{2,1,0:T(8,128)S(1)} %all-to-all-done.2.refs_0_, f32[2,64,256]{2,1,0:T(8,128)S(1)} %collective-permute-done.4.refs_1_, ...), custom_call_target="tpu_custom_call" | custom-call | flops 60000002048 | bytes 180000000 | tf_op jit(solution)/shard_map/pallas_call | solution.py:150
  56.7 3.3 %all-to-all-start.3 = ((f32[8,8,128]{2,1,0:T(8,128)}), f32[8,8,128]{2,1,0:T(8,128)S(1)}, u32[]{:S(2)}, u32[]{:S(2)}) async-start(f32[8,8,128]{2,1,0:T(8,128)} %get-tuple-element.132), calls=%async_computation.3 | async-start | bytes 65536 | tf_op jit(solution)/shard_map/all_to_all | solution.py:681
  60.0 1.9 %collective-permute-start.6 = (f32[2,64,256]{2,1,0:T(8,128)}, f32[2,64,256]{2,1,0:T(8,128)S(1)}, u32[]{:S(2)}, u32[]{:S(2)}) collective-permute-start(f32[2,64,256]{2,1,0:T(8,128)} %get-tuple-element.133), channel_id=1, source_target_pairs={{0,4},{4,8},{8,12},{12,16},{16,20},{20,24},{24,28},{28,0},{1,5},{5... | collective-permute-start | bytes 393224 | tf_op jit(solution)/shard_map/ppermute | solution.py:684
  61.9 2.9 %collective-permute-start.7 = (f32[2,64,256]{2,1,0:T(8,128)}, f32[2,64,256]{2,1,0:T(8,128)S(1)}, u32[]{:S(2)}, u32[]{:S(2)}) collective-permute-start(f32[2,64,256]{2,1,0:T(8,128)} %get-tuple-element.134), channel_id=1, source_target_pairs={{4,0},{8,4},{12,8},{16,12},{20,16},{24,20},{28,24},{0,28},{5,1},{9... | collective-permute-start | bytes 393224 | tf_op jit(solution)/shard_map/ppermute | solution.py:684
  64.8 6.1 %shard_map.147 = (f32[2,16,16384]{2,1,0:T(8,128)}, f32[128,256]{1,0:T(8,128)S(1)}, f32[2,2,64,256]{3,2,1,0:T(8,128)S(1)}, f32[2,8,128]{2,1,0:T(8,128)S(1)}, f32[...) custom-call(f32[2,16,16384]{2,1,0:T(8,128)} %get-tuple-element.115.r, ...), custom_call_target="tpu_custom_call" | custom-call | flops 60000002048 | bytes 180000000 | tf_op jit(solution)/shard_map/pallas_call | solution.py:150
  70.9 0.0 all-to-all-done.3.refs_0_
  70.9 0.0 collective-permute-done.6.refs_1_
  70.9 0.0 collective-permute-done.7.refs_2_
  70.9 1.6 %shard_map.148 = (f32[32,8,128]{2,1,0:T(8,128)}, f32[2,2,64,256]{3,2,1,0:T(8,128)}, f32[128,256]{1,0:T(8,128)}, f32[2,8,128]{2,1,0:T(8,128)}) custom-call(f32[8,8,128]{2,1,0:T(8,128)S(1)} %all-to-all-done.3.refs_0_, f32[2,64,256]{2,1,0:T(8,128)S(1)} %collective-permute-done.6.refs_1_, f32[2,64,256]{2,1,0:T(8,128)S(1)} %collective-permute-done.7.refs_2_, ...), custom_call_target="tpu_custom_call" | custom-call | flops 60000002048 | bytes 180000000 | tf_op jit(solution)/shard_map/pallas_call | solution.py:150
  72.5 3.4 %all-to-all-start.4 = ((f32[32,8,128]{2,1,0:T(8,128)}), f32[32,8,128]{2,1,0:T(8,128)S(1)}, u32[]{:S(2)}, u32[]{:S(2)}) async-start(f32[32,8,128]{2,1,0:T(8,128)} %get-tuple-element.148), calls=%async_computation.4 | async-start | bytes 262144 | tf_op jit(solution)/shard_map/all_to_all | solution.py:681
  75.9 3.6 %shard_map.149 = (f32[2,16,16384]{2,1,0:T(8,128)}, f32[2,8,128]{2,1,0:T(8,128)S(1)}, f32[6,8,128]{2,1,0:T(8,128)S(1)}) custom-call(f32[2,16,16384]{2,1,0:T(8,128)} %get-tuple-element.131.refs_0_, s32[1,8,8]{2,1,0:T(8,128)} %refs_1_.11, f32[128,256]{1,0:T(8,128)} %get-tuple-element.144.refs_2_, f32[2,2,64,256]{3,2,1,0:T(8,128)} %get-tuple-element.145.refs_3_, ...), custom_call_target="tpu_custom_call" | custom-call | flops 60000002048 | bytes 180000000 | tf_op jit(solution)/shard_map/pallas_call | solution.py:150
  79.5 4.1 %all-to-all-done.4.refs_0_ = f32[32,8,128]{2,1,0:T(8,128)S(1)} async-done(((f32[32,8,128]{2,1,0:T(8,128)}), f32[32,8,128]{2,1,0:T(8,128)S(1)}, u32[]{:S(2)}, u32[]{:S(2)}) %all-to-all-start.4) | async-done | bytes 131104 | tf_op jit(solution)/shard_map/all_to_all | solution.py:681
  83.6 1.0 %shard_map.150 = (f32[2,40]{1,0:T(2,128)}, f32[1,40]{1,0:T(1,128)}) custom-call(f32[32,8,128]{2,1,0:T(8,128)S(1)} %all-to-all-done.4.refs_0_, f32[2,8,128]{2,1,0:T(8,128)S(1)} %get-tuple-element.149.refs_1_, f32[6,8,128]{2,1,0:T(8,128)S(1)} %get-tuple-element.150.refs_2_), custom_call_target="tpu_custom_call" | custom-call | flops 60000002048 | bytes 180000000 | tf_op jit(solution)/shard_map/pallas_call | solution.py:150
Async XLA Ops:
  2.8 19.3 %collective-permute-start.1 = (f32[4,64,256]{2,1,0:T(8,128)}, f32[4,64,256]{2,1,0:T(8,128)S(1)}, u32[]{:S(2)}, u32[]{:S(2)}) collective-permute-start(f32[4,64,256]{2,1,0:T(8,128)} %get-tuple-element.82.refs_7_), channel_id=1, source_target_pairs={{0,4},{4,8},{8,12},{12,16},{16,20},{20,24},{24,28},{28,0},{1,5},{5... | collective-permute-start | bytes 786440 | tf_op jit(solution)/shard_map/ppermute | solution.py:684
  5.8 16.3 %collective-permute-start = (f32[4,64,256]{2,1,0:T(8,128)}, f32[4,64,256]{2,1,0:T(8,128)S(1)}, u32[]{:S(2)}, u32[]{:S(2)}) collective-permute-start(f32[4,64,256]{2,1,0:T(8,128)} %get-tuple-element.83.refs_8_), channel_id=1, source_target_pairs={{4,0},{8,4},{12,8},{16,12},{20,16},{24,20},{28,24},{0,28},{5,1},{9... | collective-permute-start | bytes 786440 | tf_op jit(solution)/shard_map/ppermute | solution.py:684
  12.1 10.0 %all-to-all-start = ((f32[8,8,128]{2,1,0:T(8,128)}), f32[8,8,128]{2,1,0:T(8,128)S(1)}, u32[]{:S(2)}, u32[]{:S(2)}) async-start(f32[8,8,128]{2,1,0:T(8,128)} %get-tuple-element.85), calls=%async_computation | async-start | bytes 65536 | tf_op jit(solution)/shard_map/all_to_all | solution.py:681
  23.6 15.7 %all-to-all-start.1 = ((f32[8,8,128]{2,1,0:T(8,128)}), f32[8,8,128]{2,1,0:T(8,128)S(1)}, u32[]{:S(2)}, u32[]{:S(2)}) async-start(f32[8,8,128]{2,1,0:T(8,128)} %get-tuple-element.100), calls=%async_computation.1 | async-start | bytes 65536 | tf_op jit(solution)/shard_map/all_to_all | solution.py:681
  28.4 10.8 %collective-permute-start.2 = (f32[2,64,256]{2,1,0:T(8,128)}, f32[2,64,256]{2,1,0:T(8,128)S(1)}, u32[]{:S(2)}, u32[]{:S(2)}) collective-permute-start(f32[2,64,256]{2,1,0:T(8,128)} %get-tuple-element.101), channel_id=1, source_target_pairs={{0,4},{4,8},{8,12},{12,16},{16,20},{20,24},{24,28},{28,0},{1,5},{5... | collective-permute-start | bytes 393224 | tf_op jit(solution)/shard_map/ppermute | solution.py:684
  30.4 8.8 %collective-permute-start.3 = (f32[2,64,256]{2,1,0:T(8,128)}, f32[2,64,256]{2,1,0:T(8,128)S(1)}, u32[]{:S(2)}, u32[]{:S(2)}) collective-permute-start(f32[2,64,256]{2,1,0:T(8,128)} %get-tuple-element.102), channel_id=1, source_target_pairs={{4,0},{8,4},{12,8},{16,12},{20,16},{24,20},{28,24},{0,28},{5,1},{9... | collective-permute-start | bytes 393224 | tf_op jit(solution)/shard_map/ppermute | solution.py:684
  40.9 14.2 %all-to-all-start.2 = ((f32[8,8,128]{2,1,0:T(8,128)}), f32[8,8,128]{2,1,0:T(8,128)S(1)}, u32[]{:S(2)}, u32[]{:S(2)}) async-start(f32[8,8,128]{2,1,0:T(8,128)} %get-tuple-element.116), calls=%async_computation.2 | async-start | bytes 65536 | tf_op jit(solution)/shard_map/all_to_all | solution.py:681
  44.2 10.8 %collective-permute-start.4 = (f32[2,64,256]{2,1,0:T(8,128)}, f32[2,64,256]{2,1,0:T(8,128)S(1)}, u32[]{:S(2)}, u32[]{:S(2)}) collective-permute-start(f32[2,64,256]{2,1,0:T(8,128)} %get-tuple-element.117), channel_id=1, source_target_pairs={{0,4},{4,8},{8,12},{12,16},{16,20},{20,24},{24,28},{28,0},{1,5},{5... | collective-permute-start | bytes 393224 | tf_op jit(solution)/shard_map/ppermute | solution.py:684
  46.2 8.9 %collective-permute-start.5 = (f32[2,64,256]{2,1,0:T(8,128)}, f32[2,64,256]{2,1,0:T(8,128)S(1)}, u32[]{:S(2)}, u32[]{:S(2)}) collective-permute-start(f32[2,64,256]{2,1,0:T(8,128)} %get-tuple-element.118), channel_id=1, source_target_pairs={{4,0},{8,4},{12,8},{16,12},{20,16},{24,20},{28,24},{0,28},{5,1},{9... | collective-permute-start | bytes 393224 | tf_op jit(solution)/shard_map/ppermute | solution.py:684
  56.7 14.2 %all-to-all-start.3 = ((f32[8,8,128]{2,1,0:T(8,128)}), f32[8,8,128]{2,1,0:T(8,128)S(1)}, u32[]{:S(2)}, u32[]{:S(2)}) async-start(f32[8,8,128]{2,1,0:T(8,128)} %get-tuple-element.132), calls=%async_computation.3 | async-start | bytes 65536 | tf_op jit(solution)/shard_map/all_to_all | solution.py:681
  60.0 10.9 %collective-permute-start.6 = (f32[2,64,256]{2,1,0:T(8,128)}, f32[2,64,256]{2,1,0:T(8,128)S(1)}, u32[]{:S(2)}, u32[]{:S(2)}) collective-permute-start(f32[2,64,256]{2,1,0:T(8,128)} %get-tuple-element.133), channel_id=1, source_target_pairs={{0,4},{4,8},{8,12},{12,16},{16,20},{20,24},{24,28},{28,0},{1,5},{5... | collective-permute-start | bytes 393224 | tf_op jit(solution)/shard_map/ppermute | solution.py:684
  61.9 9.0 %collective-permute-start.7 = (f32[2,64,256]{2,1,0:T(8,128)}, f32[2,64,256]{2,1,0:T(8,128)S(1)}, u32[]{:S(2)}, u32[]{:S(2)}) collective-permute-start(f32[2,64,256]{2,1,0:T(8,128)} %get-tuple-element.134), channel_id=1, source_target_pairs={{4,0},{8,4},{12,8},{16,12},{20,16},{24,20},{28,24},{0,28},{5,1},{9... | collective-permute-start | bytes 393224 | tf_op jit(solution)/shard_map/ppermute | solution.py:684
  72.5 11.1 %all-to-all-start.4 = ((f32[32,8,128]{2,1,0:T(8,128)}), f32[32,8,128]{2,1,0:T(8,128)S(1)}, u32[]{:S(2)}, u32[]{:S(2)}) async-start(f32[32,8,128]{2,1,0:T(8,128)} %get-tuple-element.148), calls=%async_computation.4 | async-start | bytes 262144 | tf_op jit(solution)/shard_map/all_to_all | solution.py:681

commit v4 on v3

--- a/solution.py
+++ b/solution.py
@@ -308,7 +308,7 @@
 def prepare_kernel(z, k):
     size = min(BLOCK, z.W)
     parts = z.W // size
-    small = k.i.seg, k.i.lake, k.i.slot, k.i.storage, k.i.area, k.i.release, k.i.link, k.i.table
+    small = k.i.storage, k.i.area, k.i.release, k.i.link, k.i.table
     load(*small)
     cls, inv = k.s.cls, k.s.inv
     columns = [pl.ds(p * size, size) for p in range(parts)]
@@ -322,8 +322,6 @@
     for n in range(1, z.NT):
         payload[n] = payload[0]
     k.o.payload.send()
-    one_hots(z, k)
-    send(k.o.near, k.o.near_edges)
     table = k.i.table.v[...]
     for p in range(parts):
         coming[p].wait()
@@ -361,10 +359,10 @@
             here = place_g + firsts[side] == segs
             on_edge[side] += jnp.sum(jnp.where(here, more, 0.0), axis=1, keepdims=True)
     for j in range(z.LT):
-        k.o.near.v[j] = jnp.where(inside == (lane_ids((z.C, LANES)) + j * LANES).astype(F32), 1.0, 0.0)
+        k.s.near[j] = jnp.where(inside == (lane_ids((z.C, LANES)) + j * LANES).astype(F32), 1.0, 0.0)
         for side in range(2):
             ids = (lane_ids((z.PR, LANES)) + j * LANES).astype(F32)
-            k.o.near_edges.v[side * z.LT + j] = jnp.where(on_edge[side] == ids, 1.0, 0.0)
+            k.s.near_edges[side * z.LT + j] = jnp.where(on_edge[side] == ids, 1.0, 0.0)
 
 
 def flow_kernel(z, k, first):
@@ -372,6 +370,8 @@
     parts = z.W // size
     inv, bed, water, rain = k.s.inv, k.s.bed, k.s.water, k.s.rain
     k.i.seg.load()
+    if first:
+        load(k.i.lake, k.i.slot)
     columns = [(pl.ds(p * size, size), pl.ds(p * size + LANES, size)) for p in range(parts)]
     if not first:
         k.i.water_c.load()
@@ -388,7 +388,13 @@
             coming[-1].append(k.copy(k.i.wet.h.at[:, :, at], water.at[:, :, inner]))
     k.pass_on()
     k.i.seg.wait()
-    if not first:
+    if first:
+        wait(k.i.lake, k.i.slot)
+        one_hots(z, k)
+        for source, here, kept in ((k.s.near, k.o.near, k.o.near_kept), (k.s.near_edges, k.o.near_edges, k.o.near_edges_kept)):
+            here.v[...] = source[...]
+            k.stores.append(k.copy(source, kept.h))
+    else:
         k.i.water_c.wait()
         whole.wait()
         scatter_contacts(z, k.i.seg.v, k.i.water_c.v, water, LANES)
@@ -695,26 +701,28 @@
     from0, from1 = swap(opened.pack0, opened.pack1)
     kept = staged_call(
         prepare_kernel, z,
-        dict(cls=Raw(rough_class), table=opened.table, seg=Scalars(contact_seg), lake=Scalars(contact_lake),
-             slot=Scalars(lake_slot), storage=storage, area=area.reshape(1, -1), release=release.reshape(1, -1),
+        dict(cls=Raw(rough_class), table=opened.table, storage=storage, area=area.reshape(1, -1), release=release.reshape(1, -1),
              link=upstream_link.reshape(1, -1)),
-        dict(payload=(z.NT, z.BR, LANES), inv=Raw((z.R, z.W)), near=near_shape, near_edges=(2 * z.LT, z.PR, LANES)),
+        dict(payload=(z.NT, z.BR, LANES), inv=Raw((z.R, z.W))),
         dict(cls=pltpu.VMEM((z.R, z.W), I32), inv=pltpu.VMEM((z.R, z.W), F32)),
         extra_sems=2 * blocks,
     )
     got = share(kept.payload, "tiles")
-    inv, near, near_edges = kept.inv, kept.near, kept.near_edges
+    inv = kept.inv
+    near_edges_shape = (2 * z.LT, z.PR, LANES)
     flow_scratch = dict(water=wide_tile, bed=wide_rows, inv=wide_rows, rain=plain_tile, out=plain_tile)
     flow_out = dict(next=Raw(tile_shape), wet_c=Here(contact_shape), edges=Here(edges_shape))
     flow = staged_call(
         functools.partial(flow_kernel, first=True), z,
-        dict(wet=Raw(depth), seg=Scalars(contact_seg), bed=Raw(bed), inv=Raw(inv), rain=Raw(rain), near=Passed(near),
-             near_edges=Passed(near_edges), own1=Passed(opened.pack1), own0=Passed(opened.pack0)),
-        dict(bed_c=Here((z.C, SEG)), bed_kept=Raw((z.C, SEG)), **flow_out),
-        dict(bed_c=pltpu.VMEM((z.C, SEG), F32), **flow_scratch),
-        extra_sems=5 * blocks + 1,
-    )
-    bed_kept = flow.bed_kept
+        dict(wet=Raw(depth), seg=Scalars(contact_seg), bed=Raw(bed), inv=Raw(inv), rain=Raw(rain), lake=Scalars(contact_lake),
+             slot=Scalars(lake_slot), own1=Passed(opened.pack1), own0=Passed(opened.pack0)),
+        dict(bed_c=Here((z.C, SEG)), bed_kept=Raw((z.C, SEG)), near=Here(near_shape), near_kept=Raw(near_shape),
+             near_edges=Here(near_edges_shape), near_edges_kept=Raw(near_edges_shape), **flow_out),
+        dict(bed_c=pltpu.VMEM((z.C, SEG), F32), near=pltpu.VMEM(near_shape, F32),
+             near_edges=pltpu.VMEM(near_edges_shape, F32), **flow_scratch),
+        extra_sems=5 * blocks + 3,
+    )
+    bed_kept, near, near_edges = flow.bed_kept, flow.near_kept, flow.near_edges_kept
 
     step_out = dict(edges=edges_shape, water_c=contact_shape, state=state_shape)
     exchange_out = dict(edge0=Raw(edge_shape), edge1=Raw(edge_shape))

time: 85.4 us -> 85.3 us (level)
  no operation moved by 1% of the time
where the time goes in v4:
time: 85.3 us; the launch traced here: 84.7 us
  Pallas kernels  39.8 us (47%)
  starting transfers between devices  38.6 us (45%)
  waiting for transfers between devices  5.22 us (6%)
  between operations  0.99 us (1%)
    pallas_call x12, Pallas kernels, staged_call(): pl.pallas_call(kernel, out_shape=[(pltpu.VMEM if here else pltpu.HBM)(x.x...  39.8 us
    all_to_all x5, starting transfers between devices, share(): return lax.all_to_all(x, axes, 0, 0, tiled=True)  18.2 us
    ppermute x4, starting transfers between devices, swap(): lax.ppermute(top, 'tiles', back)  11.5 us
    ppermute x4, starting transfers between devices, swap(): lax.ppermute(bottom, 'tiles', onward)  8.89 us
    all_to_all x5, waiting for transfers between devices, share(): return lax.all_to_all(x, axes, 0, 0, tiled=True)  5.2 us
  transfers between devices with their start and end apart: 13, of which 2 were waited for; matrix products, arithmetic and copies ran while one was open for 0% of the time, Pallas kernels for 36%

profile of v4, /device:TPU:0, one launch (start us, length us, event | category | flops | bytes accessed | tf_op | source)
XLA Modules:
  0.0 84.7 jit_solution(14290225227648440821)
XLA Ops:
  0.6 2.1 %shard_map.139 = (f32[4,64,256]{2,1,0:T(8,128)}, f32[4,64,256]{2,1,0:T(8,128)}, f32[16,128]{1,0:T(8,128)}) custom-call(f32[2,16,16384]{2,1,0:T(8,128)} %refs_0_.5, f32[16,16384]{1,0:T(8,128)} %refs_4_.7, s32[16,16384]{1,0:T(8,128)} %refs_0_.4, f32[16]{0:T(128)} %refs_3_.1), custom_call_target="tpu_custom_call" | custom-call | flops 60000002048 | bytes 180000000 | tf_op jit(solution)/shard_map/pallas_call | solution.py:150
  2.8 3.0 %collective-permute-start.1 = (f32[4,64,256]{2,1,0:T(8,128)}, f32[4,64,256]{2,1,0:T(8,128)S(1)}, u32[]{:S(2)}, u32[]{:S(2)}) collective-permute-start(f32[4,64,256]{2,1,0:T(8,128)} %get-tuple-element.80.refs_7_), channel_id=1, source_target_pairs={{0,4},{4,8},{8,12},{12,16},{16,20},{20,24},{24,28},{28,0},{1,5},{5... | collective-permute-start | bytes 786440 | tf_op jit(solution)/shard_map/ppermute | solution.py:690
  5.8 3.1 %collective-permute-start = (f32[4,64,256]{2,1,0:T(8,128)}, f32[4,64,256]{2,1,0:T(8,128)S(1)}, u32[]{:S(2)}, u32[]{:S(2)}) collective-permute-start(f32[4,64,256]{2,1,0:T(8,128)} %get-tuple-element.81.refs_8_), channel_id=1, source_target_pairs={{4,0},{8,4},{12,8},{16,12},{20,16},{24,20},{28,24},{0,28},{5,1},{9... | collective-permute-start | bytes 786440 | tf_op jit(solution)/shard_map/ppermute | solution.py:690
  8.9 3.1 %shard_map.140 = (f32[8,8,128]{2,1,0:T(8,128)}, f32[16,16384]{1,0:T(8,128)}) custom-call(s32[16,16384]{1,0:T(8,128)} %refs_0_.4, f32[16,128]{1,0:T(8,128)} %get-tuple-element.78.refs_1_, f32[2,40]{1,0:T(2,128)} %refs_2_.4, f32[1,40]{1,0:T(1,128)} %bitcast.4, f32[1,40]{1,0:T(1,128)} %bitcast.5, s32[1,40]{1,0:T(1,128)} %bitcast.6), custom_call_target="tpu_custom_call" | custom-call | flops 60000002048 | bytes 180000000 | tf_op jit(solution)/shard_map/pallas_call | solution.py:150
  12.0 3.3 %all-to-all-start = ((f32[8,8,128]{2,1,0:T(8,128)}), f32[8,8,128]{2,1,0:T(8,128)S(1)}, u32[]{:S(2)}, u32[]{:S(2)}) async-start(f32[8,8,128]{2,1,0:T(8,128)} %get-tuple-element.83), calls=%async_computation | async-start | bytes 65536 | tf_op jit(solution)/shard_map/all_to_all | solution.py:687
  15.4 5.5 %shard_map.141 = (f32[64,256]{1,0:T(8,128)S(1)}, f32[64,256]{1,0:T(8,128)}, f32[3,64,128]{2,1,0:T(8,128)S(1)}, f32[3,64,128]{2,1,0:T(8,128)}, f32[6,64,128]{2,1,...) custom-call(f32[2,16,16384]{2,1,0:T(8,128)} %refs_0_.5, ...), custom_call_target="tpu_custom_call" | custom-call | flops 60000002048 | bytes 180000000 | tf_op jit(solution)/shard_map/pallas_call | solution.py:150
  20.9 1.1 %all-to-all-done.refs_0_ = f32[8,8,128]{2,1,0:T(8,128)S(1)} async-done(((f32[8,8,128]{2,1,0:T(8,128)}), f32[8,8,128]{2,1,0:T(8,128)S(1)}, u32[]{:S(2)}, u32[]{:S(2)}) %all-to-all-start) | async-done | bytes 32800 | tf_op jit(solution)/shard_map/all_to_all | solution.py:687
  22.0 0.0 collective-permute-done.1.refs_2_
  22.0 0.0 collective-permute-done.refs_1_
  22.0 1.5 %shard_map.142 = (f32[8,8,128]{2,1,0:T(8,128)}, f32[2,4,64,256]{3,2,1,0:T(8,128)}, f32[6,8,128]{2,1,0:T(8,128)}, f32[2,2,64,256]{3,2,1,0:T(8,128)}, f32[128,256]...) custom-call(f32[8,8,128]{2,1,0:T(8,128)S(1)} %all-to-all-done.refs_0_, ...), custom_call_target="tpu_custom_call" | custom-call | flops 60000002048 | bytes 180000000 | tf_op jit(solution)/shard_map/pallas_call | solution.py:150
  23.5 4.9 %all-to-all-start.1 = ((f32[8,8,128]{2,1,0:T(8,128)}), f32[8,8,128]{2,1,0:T(8,128)S(1)}, u32[]{:S(2)}, u32[]{:S(2)}) async-start(f32[8,8,128]{2,1,0:T(8,128)} %get-tuple-element.100), calls=%async_computation.1 | async-start | bytes 65536 | tf_op jit(solution)/shard_map/all_to_all | solution.py:687
  28.3 2.0 %collective-permute-start.2 = (f32[2,64,256]{2,1,0:T(8,128)}, f32[2,64,256]{2,1,0:T(8,128)S(1)}, u32[]{:S(2)}, u32[]{:S(2)}) collective-permute-start(f32[2,64,256]{2,1,0:T(8,128)} %get-tuple-element.101), channel_id=1, source_target_pairs={{0,4},{4,8},{8,12},{12,16},{16,20},{20,24},{24,28},{28,0},{1,5},{5... | collective-permute-start | bytes 393224 | tf_op jit(solution)/shard_map/ppermute | solution.py:690
  30.3 2.7 %collective-permute-start.3 = (f32[2,64,256]{2,1,0:T(8,128)}, f32[2,64,256]{2,1,0:T(8,128)S(1)}, u32[]{:S(2)}, u32[]{:S(2)}) collective-permute-start(f32[2,64,256]{2,1,0:T(8,128)} %get-tuple-element.102), channel_id=1, source_target_pairs={{4,0},{8,4},{12,8},{16,12},{20,16},{24,20},{28,24},{0,28},{5,1},{9... | collective-permute-start | bytes 393224 | tf_op jit(solution)/shard_map/ppermute | solution.py:690
  33.1 6.1 %shard_map.143 = (f32[2,16,16384]{2,1,0:T(8,128)}, f32[128,256]{1,0:T(8,128)S(1)}, f32[2,2,64,256]{3,2,1,0:T(8,128)S(1)}, f32[2,8,128]{2,1,0:T(8,128)S(1)}, f32[...) custom-call(f32[2,16,16384]{2,1,0:T(8,128)} %get-tuple-element.82.re, ...), custom_call_target="tpu_custom_call" | custom-call | flops 60000002048 | bytes 180000000 | tf_op jit(solution)/shard_map/pallas_call | solution.py:150
  39.1 0.0 all-to-all-done.1.refs_0_
  39.2 0.0 collective-permute-done.2.refs_1_
  39.2 0.0 collective-permute-done.3.refs_2_
  39.2 1.6 %shard_map.144 = (f32[8,8,128]{2,1,0:T(8,128)}, f32[2,2,64,256]{3,2,1,0:T(8,128)}, f32[128,256]{1,0:T(8,128)}, f32[2,8,128]{2,1,0:T(8,128)}, f32[2,64,256]{2,1,0:T(8,128)}, /*index=5*/f32[2,64,256]{2,1,0:T(8,128)}) custom-call(f32[8,8,128]{2,1,0:T(8,128)S(1)} %all-to-all-done.1.refs_0_, f32[2,64,256]{2,1,0:T(8,128)S(1)} %collective-permute-done.2.refs_1_, ...), custom_call_target="tpu_custom_call" | custom-call | flops 60000002048 | bytes 180000000 | tf_op jit(solution)/shard_map/pallas_call | solution.py:150
  40.8 3.3 %all-to-all-start.2 = ((f32[8,8,128]{2,1,0:T(8,128)}), f32[8,8,128]{2,1,0:T(8,128)S(1)}, u32[]{:S(2)}, u32[]{:S(2)}) async-start(f32[8,8,128]{2,1,0:T(8,128)} %get-tuple-element.116), calls=%async_computation.2 | async-start | bytes 65536 | tf_op jit(solution)/shard_map/all_to_all | solution.py:687
  44.1 2.0 %collective-permute-start.4 = (f32[2,64,256]{2,1,0:T(8,128)}, f32[2,64,256]{2,1,0:T(8,128)S(1)}, u32[]{:S(2)}, u32[]{:S(2)}) collective-permute-start(f32[2,64,256]{2,1,0:T(8,128)} %get-tuple-element.117), channel_id=1, source_target_pairs={{0,4},{4,8},{8,12},{12,16},{16,20},{20,24},{24,28},{28,0},{1,5},{5... | collective-permute-start | bytes 393224 | tf_op jit(solution)/shard_map/ppermute | solution.py:690
  46.1 2.8 %collective-permute-start.5 = (f32[2,64,256]{2,1,0:T(8,128)}, f32[2,64,256]{2,1,0:T(8,128)S(1)}, u32[]{:S(2)}, u32[]{:S(2)}) collective-permute-start(f32[2,64,256]{2,1,0:T(8,128)} %get-tuple-element.118), channel_id=1, source_target_pairs={{4,0},{8,4},{12,8},{16,12},{20,16},{24,20},{28,24},{0,28},{5,1},{9... | collective-permute-start | bytes 393224 | tf_op jit(solution)/shard_map/ppermute | solution.py:690
  48.9 6.0 %shard_map.145 = (f32[2,16,16384]{2,1,0:T(8,128)}, f32[128,256]{1,0:T(8,128)S(1)}, f32[2,2,64,256]{3,2,1,0:T(8,128)S(1)}, f32[2,8,128]{2,1,0:T(8,128)S(1)}, f32[...) custom-call(f32[2,16,16384]{2,1,0:T(8,128)} %get-tuple-element.99.re, ...), custom_call_target="tpu_custom_call" | custom-call | flops 60000002048 | bytes 180000000 | tf_op jit(solution)/shard_map/pallas_call | solution.py:150
  55.0 0.0 all-to-all-done.2.refs_0_
  55.0 0.0 collective-permute-done.4.refs_1_
  55.0 0.0 collective-permute-done.5.refs_2_
  55.0 1.6 %shard_map.146 = (f32[8,8,128]{2,1,0:T(8,128)}, f32[2,2,64,256]{3,2,1,0:T(8,128)}, f32[128,256]{1,0:T(8,128)}, f32[2,8,128]{2,1,0:T(8,128)}, f32[2,64,256]{2,1,0:T(8,128)}, /*index=5*/f32[2,64,256]{2,1,0:T(8,128)}) custom-call(f32[8,8,128]{2,1,0:T(8,128)S(1)} %all-to-all-done.2.refs_0_, f32[2,64,256]{2,1,0:T(8,128)S(1)} %collective-permute-done.4.refs_1_, ...), custom_call_target="tpu_custom_call" | custom-call | flops 60000002048 | bytes 180000000 | tf_op jit(solution)/shard_map/pallas_call | solution.py:150
  56.6 3.3 %all-to-all-start.3 = ((f32[8,8,128]{2,1,0:T(8,128)}), f32[8,8,128]{2,1,0:T(8,128)S(1)}, u32[]{:S(2)}, u32[]{:S(2)}) async-start(f32[8,8,128]{2,1,0:T(8,128)} %get-tuple-element.132), calls=%async_computation.3 | async-start | bytes 65536 | tf_op jit(solution)/shard_map/all_to_all | solution.py:687
  60.0 1.9 %collective-permute-start.6 = (f32[2,64,256]{2,1,0:T(8,128)}, f32[2,64,256]{2,1,0:T(8,128)S(1)}, u32[]{:S(2)}, u32[]{:S(2)}) collective-permute-start(f32[2,64,256]{2,1,0:T(8,128)} %get-tuple-element.133), channel_id=1, source_target_pairs={{0,4},{4,8},{8,12},{12,16},{16,20},{20,24},{24,28},{28,0},{1,5},{5... | collective-permute-start | bytes 393224 | tf_op jit(solution)/shard_map/ppermute | solution.py:690
  61.9 2.9 %collective-permute-start.7 = (f32[2,64,256]{2,1,0:T(8,128)}, f32[2,64,256]{2,1,0:T(8,128)S(1)}, u32[]{:S(2)}, u32[]{:S(2)}) collective-permute-start(f32[2,64,256]{2,1,0:T(8,128)} %get-tuple-element.134), channel_id=1, source_target_pairs={{4,0},{8,4},{12,8},{16,12},{20,16},{24,20},{28,24},{0,28},{5,1},{9... | collective-permute-start | bytes 393224 | tf_op jit(solution)/shard_map/ppermute | solution.py:690
  64.7 6.1 %shard_map.147 = (f32[2,16,16384]{2,1,0:T(8,128)}, f32[128,256]{1,0:T(8,128)S(1)}, f32[2,2,64,256]{3,2,1,0:T(8,128)S(1)}, f32[2,8,128]{2,1,0:T(8,128)S(1)}, f32[...) custom-call(f32[2,16,16384]{2,1,0:T(8,128)} %get-tuple-element.115.r, ...), custom_call_target="tpu_custom_call" | custom-call | flops 60000002048 | bytes 180000000 | tf_op jit(solution)/shard_map/pallas_call | solution.py:150
  70.8 0.0 all-to-all-done.3.refs_0_
  70.8 0.0 collective-permute-done.6.refs_1_
  70.8 0.0 collective-permute-done.7.refs_2_
  70.8 1.6 %shard_map.148 = (f32[32,8,128]{2,1,0:T(8,128)}, f32[2,2,64,256]{3,2,1,0:T(8,128)}, f32[128,256]{1,0:T(8,128)}, f32[2,8,128]{2,1,0:T(8,128)}) custom-call(f32[8,8,128]{2,1,0:T(8,128)S(1)} %all-to-all-done.3.refs_0_, f32[2,64,256]{2,1,0:T(8,128)S(1)} %collective-permute-done.6.refs_1_, f32[2,64,256]{2,1,0:T(8,128)S(1)} %collective-permute-done.7.refs_2_, ...), custom_call_target="tpu_custom_call" | custom-call | flops 60000002048 | bytes 180000000 | tf_op jit(solution)/shard_map/pallas_call | solution.py:150
  72.4 3.4 %all-to-all-start.4 = ((f32[32,8,128]{2,1,0:T(8,128)}), f32[32,8,128]{2,1,0:T(8,128)S(1)}, u32[]{:S(2)}, u32[]{:S(2)}) async-start(f32[32,8,128]{2,1,0:T(8,128)} %get-tuple-element.148), calls=%async_computation.4 | async-start | bytes 262144 | tf_op jit(solution)/shard_map/all_to_all | solution.py:687
  75.8 3.6 %shard_map.149 = (f32[2,16,16384]{2,1,0:T(8,128)}, f32[2,8,128]{2,1,0:T(8,128)S(1)}, f32[6,8,128]{2,1,0:T(8,128)S(1)}) custom-call(f32[2,16,16384]{2,1,0:T(8,128)} %get-tuple-element.131.refs_0_, s32[1,8,8]{2,1,0:T(8,128)} %refs_1_.11, f32[128,256]{1,0:T(8,128)} %get-tuple-element.144.refs_2_, f32[2,2,64,256]{3,2,1,0:T(8,128)} %get-tuple-element.145.refs_3_, ...), custom_call_target="tpu_custom_call" | custom-call | flops 60000002048 | bytes 180000000 | tf_op jit(solution)/shard_map/pallas_call | solution.py:150
  79.5 4.1 %all-to-all-done.4.refs_0_ = f32[32,8,128]{2,1,0:T(8,128)S(1)} async-done(((f32[32,8,128]{2,1,0:T(8,128)}), f32[32,8,128]{2,1,0:T(8,128)S(1)}, u32[]{:S(2)}, u32[]{:S(2)}) %all-to-all-start.4) | async-done | bytes 131104 | tf_op jit(solution)/shard_map/all_to_all | solution.py:687
  83.6 1.0 %shard_map.150 = (f32[2,40]{1,0:T(2,128)}, f32[1,40]{1,0:T(1,128)}) custom-call(f32[32,8,128]{2,1,0:T(8,128)S(1)} %all-to-all-done.4.refs_0_, f32[2,8,128]{2,1,0:T(8,128)S(1)} %get-tuple-element.149.refs_1_, f32[6,8,128]{2,1,0:T(8,128)S(1)} %get-tuple-element.150.refs_2_), custom_call_target="tpu_custom_call" | custom-call | flops 60000002048 | bytes 180000000 | tf_op jit(solution)/shard_map/pallas_call | solution.py:150
Async XLA Ops:
  2.8 19.2 %collective-permute-start.1 = (f32[4,64,256]{2,1,0:T(8,128)}, f32[4,64,256]{2,1,0:T(8,128)S(1)}, u32[]{:S(2)}, u32[]{:S(2)}) collective-permute-start(f32[4,64,256]{2,1,0:T(8,128)} %get-tuple-element.80.refs_7_), channel_id=1, source_target_pairs={{0,4},{4,8},{8,12},{12,16},{16,20},{20,24},{24,28},{28,0},{1,5},{5... | collective-permute-start | bytes 786440 | tf_op jit(solution)/shard_map/ppermute | solution.py:690
  5.8 16.2 %collective-permute-start = (f32[4,64,256]{2,1,0:T(8,128)}, f32[4,64,256]{2,1,0:T(8,128)S(1)}, u32[]{:S(2)}, u32[]{:S(2)}) collective-permute-start(f32[4,64,256]{2,1,0:T(8,128)} %get-tuple-element.81.refs_8_), channel_id=1, source_target_pairs={{4,0},{8,4},{12,8},{16,12},{20,16},{24,20},{28,24},{0,28},{5,1},{9... | collective-permute-start | bytes 786440 | tf_op jit(solution)/shard_map/ppermute | solution.py:690
  12.0 10.0 %all-to-all-start = ((f32[8,8,128]{2,1,0:T(8,128)}), f32[8,8,128]{2,1,0:T(8,128)S(1)}, u32[]{:S(2)}, u32[]{:S(2)}) async-start(f32[8,8,128]{2,1,0:T(8,128)} %get-tuple-element.83), calls=%async_computation | async-start | bytes 65536 | tf_op jit(solution)/shard_map/all_to_all | solution.py:687
  23.5 15.7 %all-to-all-start.1 = ((f32[8,8,128]{2,1,0:T(8,128)}), f32[8,8,128]{2,1,0:T(8,128)S(1)}, u32[]{:S(2)}, u32[]{:S(2)}) async-start(f32[8,8,128]{2,1,0:T(8,128)} %get-tuple-element.100), calls=%async_computation.1 | async-start | bytes 65536 | tf_op jit(solution)/shard_map/all_to_all | solution.py:687
  28.3 10.8 %collective-permute-start.2 = (f32[2,64,256]{2,1,0:T(8,128)}, f32[2,64,256]{2,1,0:T(8,128)S(1)}, u32[]{:S(2)}, u32[]{:S(2)}) collective-permute-start(f32[2,64,256]{2,1,0:T(8,128)} %get-tuple-element.101), channel_id=1, source_target_pairs={{0,4},{4,8},{8,12},{12,16},{16,20},{20,24},{24,28},{28,0},{1,5},{5... | collective-permute-start | bytes 393224 | tf_op jit(solution)/shard_map/ppermute | solution.py:690
  30.3 8.8 %collective-permute-start.3 = (f32[2,64,256]{2,1,0:T(8,128)}, f32[2,64,256]{2,1,0:T(8,128)S(1)}, u32[]{:S(2)}, u32[]{:S(2)}) collective-permute-start(f32[2,64,256]{2,1,0:T(8,128)} %get-tuple-element.102), channel_id=1, source_target_pairs={{4,0},{8,4},{12,8},{16,12},{20,16},{24,20},{28,24},{0,28},{5,1},{9... | collective-permute-start | bytes 393224 | tf_op jit(solution)/shard_map/ppermute | solution.py:690
  40.8 14.2 %all-to-all-start.2 = ((f32[8,8,128]{2,1,0:T(8,128)}), f32[8,8,128]{2,1,0:T(8,128)S(1)}, u32[]{:S(2)}, u32[]{:S(2)}) async-start(f32[8,8,128]{2,1,0:T(8,128)} %get-tuple-element.116), calls=%async_computation.2 | async-start | bytes 65536 | tf_op jit(solution)/shard_map/all_to_all | solution.py:687
  44.1 10.8 %collective-permute-start.4 = (f32[2,64,256]{2,1,0:T(8,128)}, f32[2,64,256]{2,1,0:T(8,128)S(1)}, u32[]{:S(2)}, u32[]{:S(2)}) collective-permute-start(f32[2,64,256]{2,1,0:T(8,128)} %get-tuple-element.117), channel_id=1, source_target_pairs={{0,4},{4,8},{8,12},{12,16},{16,20},{20,24},{24,28},{28,0},{1,5},{5... | collective-permute-start | bytes 393224 | tf_op jit(solution)/shard_map/ppermute | solution.py:690
  46.1 8.9 %collective-permute-start.5 = (f32[2,64,256]{2,1,0:T(8,128)}, f32[2,64,256]{2,1,0:T(8,128)S(1)}, u32[]{:S(2)}, u32[]{:S(2)}) collective-permute-start(f32[2,64,256]{2,1,0:T(8,128)} %get-tuple-element.118), channel_id=1, source_target_pairs={{4,0},{8,4},{12,8},{16,12},{20,16},{24,20},{28,24},{0,28},{5,1},{9... | collective-permute-start | bytes 393224 | tf_op jit(solution)/shard_map/ppermute | solution.py:690
  56.6 14.2 %all-to-all-start.3 = ((f32[8,8,128]{2,1,0:T(8,128)}), f32[8,8,128]{2,1,0:T(8,128)S(1)}, u32[]{:S(2)}, u32[]{:S(2)}) async-start(f32[8,8,128]{2,1,0:T(8,128)} %get-tuple-element.132), calls=%async_computation.3 | async-start | bytes 65536 | tf_op jit(solution)/shard_map/all_to_all | solution.py:687
  60.0 10.9 %collective-permute-start.6 = (f32[2,64,256]{2,1,0:T(8,128)}, f32[2,64,256]{2,1,0:T(8,128)S(1)}, u32[]{:S(2)}, u32[]{:S(2)}) collective-permute-start(f32[2,64,256]{2,1,0:T(8,128)} %get-tuple-element.133), channel_id=1, source_target_pairs={{0,4},{4,8},{8,12},{12,16},{16,20},{20,24},{24,28},{28,0},{1,5},{5... | collective-permute-start | bytes 393224 | tf_op jit(solution)/shard_map/ppermute | solution.py:690
  61.9 9.0 %collective-permute-start.7 = (f32[2,64,256]{2,1,0:T(8,128)}, f32[2,64,256]{2,1,0:T(8,128)S(1)}, u32[]{:S(2)}, u32[]{:S(2)}) collective-permute-start(f32[2,64,256]{2,1,0:T(8,128)} %get-tuple-element.134), channel_id=1, source_target_pairs={{4,0},{8,4},{12,8},{16,12},{20,16},{24,20},{28,24},{0,28},{5,1},{9... | collective-permute-start | bytes 393224 | tf_op jit(solution)/shard_map/ppermute | solution.py:690
  72.4 11.1 %all-to-all-start.4 = ((f32[32,8,128]{2,1,0:T(8,128)}), f32[32,8,128]{2,1,0:T(8,128)S(1)}, u32[]{:S(2)}, u32[]{:S(2)}) async-start(f32[32,8,128]{2,1,0:T(8,128)} %get-tuple-element.148), calls=%async_computation.4 | async-start | bytes 262144 | tf_op jit(solution)/shard_map/all_to_all | solution.py:687
